TPU v7x, 256 devices: a whole 4x4x8 slice. The times are simulated.
256 devices in a mesh: cohort: 32 (over x, y, core), snp: 8 (over z).
Axes of the slice: x: 4, y: 4, z: 8, core: 2. Of those that a mesh axis runs over, the one named last changes fastest.
Arguments:
- rhs_animal: float32 [4, 262144], P(None, 'cohort'), may hold values from -40 to 40
- rhs_snp: float32 [4, 51200], P(None, 'snp'), may hold values from -6 to 6
- record_weight: float32 [262144], P('cohort'), may hold values from 0.5 to 2
- sire_index: int32 [262144], P('cohort'), may hold values from -1 to 253951, as said below
- dam_index: int32 [262144], P('cohort'), may hold values from -1 to 253951, as said below
- cohort_sizes: int32 [32], replicated, may hold values from 2048 to 8192, as said below
- geno_index: int32 [8192], P('cohort'), may hold values from 0 to 262143, as said below
- genotypes: float32 [8192, 51200], P('cohort', 'snp'), may hold values from -0.0625 to 0.0625
- precond_animal: float32 [4, 4, 262144], P(None, None, 'cohort'), may hold values from -0.3 to 3, as said below
- precond_snp: float32 [4, 4, 51200], P(None, None, 'snp'), may hold values from -0.3 to 2, as said below
- genetic_inv: float32 [4, 4], replicated, may hold values from -0.3 to 2, as said below
- residual_inv: float32 [4, 4], replicated, may hold values from -0.3 to 2, as said below
- coupling: float32 [4, 4], replicated, may hold values from -0.3 to 2, as said below
- snp_prior: float32 [4, 4], replicated, may hold values from -0.3 to 2, as said below
Outputs:
- solution_animal: float32 [4, 262144], P(None, 'cohort')
- solution_snp: float32 [4, 51200], P(None, 'snp')
- residual_animal: float32 [4, 262144], P(None, 'cohort')
- residual_snp: float32 [4, 51200], P(None, 'snp')
Inputs may be any that keep to these rules, and one draw needn't show every extreme that they name: `cohort_sizes`: some cohort has exactly 8192 live animals. `sire_index`: -1, or a live animal born 1 to 3 cohorts before the animal; animals in empty slots have -1. `dam_index`: -1, or a live animal born 1 to 3 cohorts before the animal; animals in empty slots have -1. `geno_index`: entries c * 256 to (c + 1) * 256 - 1 are distinct live animals of cohort c, in rising order. `precond_animal`: each block is symmetric with a dominant diagonal. `precond_snp`: each block is symmetric with a dominant diagonal. `genetic_inv`: symmetric with a dominant diagonal. `residual_inv`: symmetric with a dominant diagonal. `coupling`: symmetric with a dominant diagonal. `snp_prior`: symmetric with a dominant diagonal.
All inputs are finite; a program needn't handle non-finite values.
Results may differ from a plain program's by a relative error of at most 0.00012.
Values sent between devices are 32-bit elements; how exact they have to be, the bound alone decides.
A program may use at most 128 MiB of HBM per device.

v0:
```python
import jax
import jax.numpy as jnp
from jax import lax
from jax.sharding import PartitionSpec as P

SPAN = 3
ITERS = 2


def shifted(block, axis, distance):
    devices = range(lax.axis_size(axis))
    route = [(i - distance, i) for i in devices if i - distance in devices]
    return lax.ppermute(block, axis, route)


def matmul(left, right):
    return jnp.dot(left, right, precision=lax.Precision.HIGHEST)


def precondition(blocks, field):
    return jnp.sum(blocks * field[None, :, :], axis=1)


def body(
    rhs_animal,
    rhs_snp,
    record_weight,
    sire_index,
    dam_index,
    cohort_sizes,
    geno_index,
    genotypes,
    precond_animal,
    precond_snp,
    genetic_inv,
    residual_inv,
    coupling,
    snp_prior,
):
    traits, block_len = rhs_animal.shape
    cohort_pos = lax.axis_index("cohort")
    snp_pos = lax.axis_index("snp")
    first_animal = cohort_pos * block_len
    slots = jnp.arange(block_len, dtype=jnp.int32)
    live_count = jnp.sum(
        jnp.where(jnp.arange(cohort_sizes.shape[0], dtype=jnp.int32) == cohort_pos, cohort_sizes, 0)
    )
    live = (slots < live_count).astype(jnp.float32)

    def parent_slots(parent):
        lag = cohort_pos - parent // block_len
        local = (lag - 1) * block_len + parent % block_len
        return jnp.where(parent >= 0, local, SPAN * block_len)

    sire_pos = parent_slots(sire_index)
    dam_pos = parent_slots(dam_index)
    known = (sire_index >= 0).astype(jnp.float32) + (dam_index >= 0).astype(jnp.float32)
    factor = 4.0 / (4.0 - known)
    geno_local = geno_index - first_animal

    def earlier_blocks(field):
        return [shifted(field, "cohort", lag) for lag in range(1, SPAN + 1)]

    def later_terms(terms):
        total = jnp.zeros((traits, block_len), jnp.float32)
        for lag in range(1, SPAN + 1):
            total = total + shifted(terms[lag - 1], "cohort", -lag)
        return total

    def pedigree_inverse(field):
        blocks = earlier_blocks(field)
        stacked = jnp.concatenate(blocks + [jnp.zeros((traits, 1), jnp.float32)], axis=1)
        mendel = factor * (field - 0.5 * stacked[:, sire_pos] - 0.5 * stacked[:, dam_pos])
        back = jnp.zeros((traits, SPAN * block_len + 1), jnp.float32)
        back = back.at[:, sire_pos].add(-0.5 * mendel).at[:, dam_pos].add(-0.5 * mendel)
        terms = [back[:, lag * block_len : (lag + 1) * block_len] for lag in range(SPAN)]
        return mendel + later_terms(terms)

    def local_inner(left_a, left_s, right_a, right_s):
        animal_part = jnp.where(snp_pos == 0, jnp.sum(left_a * right_a), 0.0)
        marker_part = jnp.where(cohort_pos == 0, jnp.sum(left_s * right_s), 0.0)
        return animal_part + marker_part

    def precond_inner(res_a, res_s, pre_a, pre_s):
        return lax.psum(local_inner(res_a, res_s, pre_a, pre_s), ("cohort", "snp"))

    res_animal = rhs_animal * live[None, :]
    res_snp = rhs_snp
    sol_animal = jnp.zeros_like(res_animal)
    sol_snp = jnp.zeros_like(res_snp)
    pre_animal = precondition(precond_animal, res_animal)
    pre_snp = precondition(precond_snp, res_snp)
    dir_animal, dir_snp = (pre_animal, pre_snp)
    gamma = precond_inner(res_animal, res_snp, pre_animal, pre_snp)
    for step in range(ITERS):
        partial_sums = lax.dot_general(
            dir_snp, genotypes, (((1,), (1,)), ((), ())), precision=lax.Precision.HIGHEST
        )
        marker_sums = lax.psum(partial_sums, "snp")
        tied = matmul(coupling, dir_animal[:, geno_local] - marker_sums)
        pedigree = pedigree_inverse(dir_animal)
        snp_part = lax.psum(matmul(tied, genotypes), "cohort")
        out_animal = record_weight[None, :] * matmul(residual_inv, dir_animal) + matmul(
            genetic_inv, pedigree
        )
        out_animal = out_animal.at[:, geno_local].add(tied)
        out_snp = matmul(snp_prior, dir_snp) - snp_part
        alpha = gamma / lax.psum(
            local_inner(dir_animal, dir_snp, out_animal, out_snp), ("cohort", "snp")
        )
        sol_animal = sol_animal + alpha * dir_animal
        sol_snp = sol_snp + alpha * dir_snp
        res_animal = res_animal - alpha * out_animal
        res_snp = res_snp - alpha * out_snp
        if step + 1 < ITERS:
            pre_animal = precondition(precond_animal, res_animal)
            pre_snp = precondition(precond_snp, res_snp)
            gamma_new = precond_inner(res_animal, res_snp, pre_animal, pre_snp)
            dir_animal = pre_animal + gamma_new / gamma * dir_animal
            dir_snp = pre_snp + gamma_new / gamma * dir_snp
            gamma = gamma_new
    return (sol_animal, sol_snp, res_animal, res_snp)


def solution(mesh):
    in_specs = (
        P(None, "cohort"),
        P(None, "snp"),
        P("cohort"),
        P("cohort"),
        P("cohort"),
        P(),
        P("cohort"),
        P("cohort", "snp"),
        P(None, None, "cohort"),
        P(None, None, "snp"),
        P(),
        P(),
        P(),
        P(),
    )
    out_specs = (P(None, "cohort"), P(None, "snp"), P(None, "cohort"), P(None, "snp"))
    return jax.shard_map(body, mesh=mesh, in_specs=in_specs, out_specs=out_specs, check_vma=False)
```

profile of v0, /device:TPU:1, one launch (start us, length us, event | category | flops | bytes accessed | tf_op | source)
XLA Modules:
  0.0 871.7 jit_solution(17051540248849357471)
XLA Ops:
  11.6 6.2 collective-permute-start.2
  25.3 7.2 fusion.42
  32.6 16.3 %psum.57 = f32[4,256]{1,0:T(4,128)S(1)} all-reduce(f32[4,256]{1,0:T(4,128)S(1)} %fusion.42), channel_id=1, replica_groups=mesh['cohort'=32,'snp'=8] {'snp'}, use_global_device_ids=true, to_apply=%region_8.9 | all-reduce | flops 1024 | bytes 8192 | tf_op jit(solution)/shard_map/psum | solution.py:99
  48.9 2.9 gather_fusion.2
  52.0 6.7 fusion.43
  59.8 7.0 copy.93
  66.8 32.4 %gather_fusion.1 = f32[8192,4]{1,0:T(8,128)} fusion(f32[4,24577]{0,1:T(8,128)} %copy.93, s32[8192]{0:T(1024)S(1)} %get-tuple-element.22), kind=kCustom, calls=%fused_computation.1 | custom fusion | bytes 294912 | tf_op jit(solution)/shard_map/gather | solution.py:73
  99.2 4.4 broadcast_multiply_fusion.2
  103.6 2.8 copy.124
  106.4 32.5 %gather_fusion = f32[8192,4]{1,0:T(8,128)} fusion(f32[4,24577]{0,1:T(8,128)} %copy.93, s32[8192]{0:T(1024)S(1)} %get-tuple-element.34), kind=kCustom, calls=%fused_computation | custom fusion | bytes 294912 | tf_op jit(solution)/shard_map/gather | solution.py:73
  138.9 4.4 broadcast_multiply_fusion.3
  143.3 2.9 copy.123
  149.5 57.5 %scatter_custom_fusion = f32[4,24577]{0,1:T(8,128)} fusion(s32[8192]{0:T(1024)S(1)} %get-tuple-element.35, f32[8192,4]{1,0:T(8,128)} %copy.97, f32[]{:T(128)} %constant.60.clone.1), kind=kCustom, calls=%fused_computation.24 | custom fusion | flops 32768 | bytes 393744 | tf_op jit(solution)/shard_map/scatter-add | solution.py:75
  207.0 60.9 %scatter_fusion = f32[4,24577]{0,1:T(8,128)} fusion(f32[4,24577]{0,1:T(8,128)} %scatter_custom_fusion, s32[8192]{0:T(1024)S(1)} %get-tuple-element.23, f32[8192,4]{1,0:T(8,128)} %copy.97), kind=kCustom, calls=%fused_computation.7 | custom fusion | flops 32768 | bytes 425984 | tf_op jit(solution)/shard_map/scatter-add | solution.py:75
  267.9 9.5 %fusion.41 = (f32[4,8192]{0,1:T(8,128)}, f32[4,8192]{0,1:T(8,128)}, f32[4,8192]{0,1:T(8,128)}) fusion(f32[4,24577]{0,1:T(8,128)} %scatter_fusion), kind=kLoop, calls=%fused_computation.115 | loop fusion | bytes 786432 | tf_op jit(solution)/shard_map/slice | solution.py:76
  277.4 2.8 copy.101
  281.6 2.9 copy.99
  284.5 16.5 %collective-permute-start.3 = (f32[4,8192]{1,0:T(4,128)S(1)}, f32[4,8192]{1,0:T(4,128)S(1)}, u32[]{:S(2)}, u32[]{:S(2)}) collective-permute-start(f32[4,8192]{1,0:T(4,128)S(1)} %copy.99), channel_id=1, source_target_pairs={{8,0},{16,8},{24,16},{32,24},{40,32},{48,40},{56,48},{64,56},{72,6... | collective-permute-start | bytes 393224 | tf_op jit(solution)/shard_map/ppermute | solution.py:13
  301.0 2.8 copy.100
  313.8 5.9 scatter_fusion.1
  319.7 5.1 multiply_reduce_fusion
  325.5 2.8 copy.107
  328.4 74.4 %all-reduce = (f32[]{:T(128)}, f32[]{:T(128)}) all-reduce(f32[]{:T(128)S(6)} %add.123, f32[]{:T(128)S(6)} %add.137), channel_id=1, replica_groups=mesh['cohort'=32,'snp'=8] {'cohort','snp'}, use_global_device_ids=true, to_apply=%region_5.6 | all-reduce | flops 2 | bytes 16 | tf_op jit(solution)/shard_map/psum | solution.py:85
  407.5 73.3 %psum.60 = f32[]{:T(128)} all-reduce(f32[]{:T(128)S(6)} %add.138), channel_id=1, replica_groups=mesh['cohort'=32,'snp'=8] {'cohort','snp'}, use_global_device_ids=true, to_apply=%region_18.19 | all-reduce | flops 1 | bytes 8 | tf_op jit(solution)/shard_map/psum | solution.py:85
  482.1 3.7 collective-permute-start.8
  485.8 3.0 collective-permute-start.7
  493.7 7.2 fusion.44
  500.9 12.0 %psum.61 = f32[4,256]{1,0:T(4,128)S(1)} all-reduce(f32[4,256]{1,0:T(4,128)S(1)} %fusion.44), channel_id=1, replica_groups=mesh['cohort'=32,'snp'=8] {'snp'}, use_global_device_ids=true, to_apply=%region_21.22 | all-reduce | flops 1024 | bytes 8192 | tf_op jit(solution)/shard_map/psum | solution.py:99
  512.9 2.9 gather_fusion.5
  516.2 6.7 fusion.45
  523.4 7.0 copy.108
  530.4 32.4 %gather_fusion.4 = f32[8192,4]{1,0:T(8,128)} fusion(f32[4,24577]{0,1:T(8,128)} %copy.108, s32[8192]{0:T(1024)S(1)} %get-tuple-element.22), kind=kCustom, calls=%fused_computation.4 | custom fusion | bytes 294912 | tf_op jit(solution)/shard_map/gather | solution.py:73
  562.9 32.5 %gather_fusion.3 = f32[8192,4]{1,0:T(8,128)} fusion(f32[4,24577]{0,1:T(8,128)} %copy.108, s32[8192]{0:T(1024)S(1)} %get-tuple-element.34), kind=kCustom, calls=%fused_computation.3 | custom fusion | bytes 294912 | tf_op jit(solution)/shard_map/gather | solution.py:73
  595.4 4.4 broadcast_multiply_fusion
  599.8 2.8 copy.126
  602.6 4.4 broadcast_multiply_fusion.1
  607.0 2.9 copy.125
  612.6 57.5 %scatter_custom_fusion.3 = f32[4,24577]{0,1:T(8,128)} fusion(s32[8192]{0:T(1024)S(1)} %get-tuple-element.35, f32[8192,4]{1,0:T(8,128)} %copy.112, f32[]{:T(128)} %constant.60.clone.1), kind=kCustom, calls=%fused_computation.22 | custom fusion | flops 32768 | bytes 393744 | tf_op jit(solution)/shard_map/scatter-add | solution.py:75
  670.1 61.1 %scatter_fusion.2 = f32[4,24577]{0,1:T(8,128)} fusion(f32[4,24577]{0,1:T(8,128)} %scatter_custom_fusion.3, s32[8192]{0:T(1024)S(1)} %get-tuple-element.23, f32[8192,4]{1,0:T(8,128)} %copy.112), kind=kCustom, calls=%fused_computation.10 | custom fusion | flops 32768 | bytes 425984 | tf_op jit(solution)/shard_map/scatter-add | solution.py:75
  731.2 9.4 %fusion.40 = (f32[4,8192]{0,1:T(8,128)}, f32[4,8192]{0,1:T(8,128)}, f32[4,8192]{0,1:T(8,128)}) fusion(f32[4,24577]{0,1:T(8,128)} %scatter_fusion.2), kind=kLoop, calls=%fused_computation.114 | loop fusion | bytes 786432 | tf_op jit(solution)/shard_map/slice | solution.py:76
  740.6 2.8 copy.116
  744.8 2.8 copy.114
  747.6 16.5 %collective-permute-start.9 = (f32[4,8192]{1,0:T(4,128)S(1)}, f32[4,8192]{1,0:T(4,128)S(1)}, u32[]{:S(2)}, u32[]{:S(2)}) collective-permute-start(f32[4,8192]{1,0:T(4,128)S(1)} %copy.114), channel_id=1, source_target_pairs={{8,0},{16,8},{24,16},{32,24},{40,32},{48,40},{56,48},{64,56},{72,6... | collective-permute-start | bytes 393224 | tf_op jit(solution)/shard_map/ppermute | solution.py:13
  764.1 2.8 copy.115
  770.8 3.1 collective-permute-done.10
  776.9 5.9 scatter_fusion.3
  782.8 2.8 copy.121
  787.0 73.6 %psum.63 = f32[]{:T(128)} all-reduce(f32[]{:T(128)S(6)} %add.146), channel_id=1, replica_groups=mesh['cohort'=32,'snp'=8] {'cohort','snp'}, use_global_device_ids=true, to_apply=%region_26.27 | all-reduce | flops 1 | bytes 8 | tf_op jit(solution)/shard_map/psum | solution.py:108
  (93 shorter events, 47.1 us)
Async XLA Ops:
  7.2 51.9 %copy-start = (f32[4,4]{1,0:T(4,128)S(1)}, f32[4,4]{1,0:T(4,128)}, u32[]{:S(2)}) copy-start(f32[4,4]{1,0:T(4,128)} %param.25) | copy-start | bytes 196
  7.2 17.8 %copy-start.2 = (f32[4,4,6400]{2,1,0:T(4,128)S(1)}, f32[4,4,6400]{2,1,0:T(4,128)}, u32[]{:S(2)}) copy-start(f32[4,4,6400]{2,1,0:T(4,128)} %param.23) | copy-start | bytes 1228804
  7.2 17.8 %copy-start.4 = (f32[4,6400]{1,0:T(4,128)S(1)}, f32[4,6400]{1,0:T(4,128)}, u32[]{:S(2)}) copy-start(f32[4,6400]{1,0:T(4,128)} %param.15) | copy-start | bytes 307204
  7.2 298.1 %all-reduce.4.cloned.1.call-start = ((), (), s32[]{:S(2)}) async-start(), calls=%async_computation | async-start | bytes 204800 | tf_op jit(solution)/shard_map/psum | solution.py:102
  11.6 48.0 %collective-permute-start.2 = (f32[4,8192]{1,0:T(4,128)S(1)}, f32[4,8192]{1,0:T(4,128)S(1)}, u32[]{:S(2)}, u32[]{:S(2)}) collective-permute-start(f32[4,8192]{1,0:T(4,128)S(1)} %multiply_reduce_fusion.2), channel_id=1, source_target_pairs={{0,24},{8,32},{16,40},{24,48},{32,56},{40,64},{48,72},{56,80},{64,... | collective-permute-start | bytes 393224 | tf_op jit(solution)/shard_map/ppermute | solution.py:13
  17.8 41.8 %collective-permute-start.1 = (f32[4,8192]{1,0:T(4,128)S(1)}, f32[4,8192]{1,0:T(4,128)S(1)}, u32[]{:S(2)}, u32[]{:S(2)}) collective-permute-start(f32[4,8192]{1,0:T(4,128)S(1)} %multiply_reduce_fusion.2), channel_id=1, source_target_pairs={{0,16},{8,24},{16,32},{24,40},{32,48},{40,56},{48,64},{56,72},{64,... | collective-permute-start | bytes 393224 | tf_op jit(solution)/shard_map/ppermute | solution.py:13
  20.2 39.5 %collective-permute-start = (f32[4,8192]{1,0:T(4,128)S(1)}, f32[4,8192]{1,0:T(4,128)S(1)}, u32[]{:S(2)}, u32[]{:S(2)}) collective-permute-start(f32[4,8192]{1,0:T(4,128)S(1)} %multiply_reduce_fusion.2), channel_id=1, source_target_pairs={{0,8},{8,16},{16,24},{24,32},{32,40},{40,48},{48,56},{56,64},{64,7... | collective-permute-start | bytes 393224 | tf_op jit(solution)/shard_map/ppermute | solution.py:13
  25.0 23.8 %copy-start.11 = (s32[256]{0:T(256)S(1)}, s32[256]{0:T(256)}, u32[]{:S(2)}) copy-start(s32[256]{0:T(256)} %param.20) | copy-start | bytes 3076
  25.0 26.8 %copy-start.10 = (f32[4,4]{1,0:T(4,128)S(1)}, f32[4,4]{1,0:T(4,128)}, u32[]{:S(2)}) copy-start(f32[4,4]{1,0:T(4,128)} %param.26) | copy-start | bytes 196
  32.5 26.5 %copy-start.5 = (f32[8192]{0:T(1024)S(1)}, f32[8192]{0:T(1024)}, u32[]{:S(2)}) copy-start(f32[8192]{0:T(1024)} %param.16) | copy-start | bytes 98308
  32.6 26.9 %copy-start.6 = (s32[8192]{0:T(1024)S(1)}, s32[8192]{0:T(1024)}, u32[]{:S(2)}) copy-start(s32[8192]{0:T(1024)} %param.18) | copy-start | bytes 98308
  32.6 26.9 %copy-start.7 = (s32[8192]{0:T(1024)S(1)}, s32[8192]{0:T(1024)}, u32[]{:S(2)}) copy-start(s32[8192]{0:T(1024)} %param.17) | copy-start | bytes 98308
  58.7 709.6 %all-reduce.6.cloned.1.call-start = ((), (), s32[]{:S(2)}) async-start(), calls=%async_computation.1 | async-start | bytes 204800 | tf_op jit(solution)/shard_map/psum | solution.py:102
  143.3 2.9 copy-start.3
  280.3 28.9 %collective-permute-start.5 = (f32[4,8192]{1,0:T(4,128)S(1)}, f32[4,8192]{1,0:T(4,128)S(1)}, u32[]{:S(2)}, u32[]{:S(2)}) collective-permute-start(f32[4,8192]{1,0:T(4,128)S(1)} %copy.101), channel_id=1, source_target_pairs={{24,0},{32,8},{40,16},{48,24},{56,32},{64,40},{72,48},{80,56},{88,... | collective-permute-start | bytes 393224 | tf_op jit(solution)/shard_map/ppermute | solution.py:13
  281.6 23.8 %copy-start.8 = (f32[4,4]{1,0:T(4,128)S(1)}, f32[4,4]{1,0:T(4,128)}, u32[]{:S(2)}) copy-start(f32[4,4]{1,0:T(4,128)} %param.27) | copy-start | bytes 196
  281.6 29.2 %copy-start.9 = (f32[4,4]{1,0:T(4,128)S(1)}, f32[4,4]{1,0:T(4,128)}, u32[]{:S(2)}) copy-start(f32[4,4]{1,0:T(4,128)} %param.24) | copy-start | bytes 196
  284.5 24.7 %collective-permute-start.3 = (f32[4,8192]{1,0:T(4,128)S(1)}, f32[4,8192]{1,0:T(4,128)S(1)}, u32[]{:S(2)}, u32[]{:S(2)}) collective-permute-start(f32[4,8192]{1,0:T(4,128)S(1)} %copy.99), channel_id=1, source_target_pairs={{8,0},{16,8},{24,16},{32,24},{40,32},{48,40},{56,48},{64,56},{72,6... | collective-permute-start | bytes 393224 | tf_op jit(solution)/shard_map/ppermute | solution.py:13
  303.8 7.0 collective-permute-start.4
  324.8 79.3 %copy-start.1 = (f32[4,4,8192]{2,1,0:T(4,128)S(1)}, f32[4,4,8192]{2,1,0:T(4,128)}, u32[]{:S(2)}) copy-start(f32[4,4,8192]{2,1,0:T(4,128)} %param.22) | copy-start | bytes 1572868
  482.1 41.1 %collective-permute-start.8 = (f32[4,8192]{1,0:T(4,128)S(1)}, f32[4,8192]{1,0:T(4,128)S(1)}, u32[]{:S(2)}, u32[]{:S(2)}) collective-permute-start(f32[4,8192]{1,0:T(4,128)S(1)} %multiply_add_fusion.1), channel_id=1, source_target_pairs={{0,24},{8,32},{16,40},{24,48},{32,56},{40,64},{48,72},{56,80},{64,... | collective-permute-start | bytes 393224 | tf_op jit(solution)/shard_map/ppermute | solution.py:13
  485.8 37.5 %collective-permute-start.7 = (f32[4,8192]{1,0:T(4,128)S(1)}, f32[4,8192]{1,0:T(4,128)S(1)}, u32[]{:S(2)}, u32[]{:S(2)}) collective-permute-start(f32[4,8192]{1,0:T(4,128)S(1)} %multiply_add_fusion.1), channel_id=1, source_target_pairs={{0,16},{8,24},{16,32},{24,40},{32,48},{40,56},{48,64},{56,72},{64,... | collective-permute-start | bytes 393224 | tf_op jit(solution)/shard_map/ppermute | solution.py:13
  488.8 34.4 %collective-permute-start.6 = (f32[4,8192]{1,0:T(4,128)S(1)}, f32[4,8192]{1,0:T(4,128)S(1)}, u32[]{:S(2)}, u32[]{:S(2)}) collective-permute-start(f32[4,8192]{1,0:T(4,128)S(1)} %multiply_add_fusion.1), channel_id=1, source_target_pairs={{0,8},{8,16},{16,24},{24,32},{32,40},{40,48},{48,56},{56,64},{64,7... | collective-permute-start | bytes 393224 | tf_op jit(solution)/shard_map/ppermute | solution.py:13
  743.5 27.3 %collective-permute-start.11 = (f32[4,8192]{1,0:T(4,128)S(1)}, f32[4,8192]{1,0:T(4,128)S(1)}, u32[]{:S(2)}, u32[]{:S(2)}) collective-permute-start(f32[4,8192]{1,0:T(4,128)S(1)} %copy.116), channel_id=1, source_target_pairs={{24,0},{32,8},{40,16},{48,24},{56,32},{64,40},{72,48},{80,56},{88,... | collective-permute-start | bytes 393224 | tf_op jit(solution)/shard_map/ppermute | solution.py:13
  747.6 23.2 %collective-permute-start.9 = (f32[4,8192]{1,0:T(4,128)S(1)}, f32[4,8192]{1,0:T(4,128)S(1)}, u32[]{:S(2)}, u32[]{:S(2)}) collective-permute-start(f32[4,8192]{1,0:T(4,128)S(1)} %copy.114), channel_id=1, source_target_pairs={{8,0},{16,8},{24,16},{32,24},{40,32},{48,40},{56,48},{64,56},{72,6... | collective-permute-start | bytes 393224 | tf_op jit(solution)/shard_map/ppermute | solution.py:13
  766.9 7.0 collective-permute-start.10
Sparse Core Ops, SparseCore 0:
  58.8 110.3 all-reduce.3
  523.0 108.5 all-reduce.5
where the time goes:
time: 879 us; the launch traced here: 872 us
  other arithmetic  283 us (32%)
  blocking collectives  250 us (28%)
  local copies, waits for them, and re-layouts  219 us (25%)
  starting transfers between devices  58.2 us (7%)
  matrix products  33.1 us (4%)
  between operations  24 us (3%)
    scatter-add x4, other arithmetic, pedigree_inverse(): back.at[:, sire_pos].add(-0.5 * mendel).at[:, dam_pos].add(-0.5 * mendel)  237 us
    psum x2, blocking collectives, precond_inner(): return lax.psum(local_inner(res_a, res_s, pre_a, pre_s), ('cohort', 'snp'))  148 us
    psum x1, blocking collectives, body(): lax.psum(local_inner(dir_animal, dir_snp, out_animal, out_snp), ('cohort'...  73.6 us
    gather x2, local copies, waits for them, and re-layouts, pedigree_inverse(): stacked[:, sire_pos]  65 us
    gather x2, local copies, waits for them, and re-layouts, pedigree_inverse(): stacked[:, dam_pos]  64.9 us
    ppermute x12, starting transfers between devices, shifted(): return lax.ppermute(block, axis, route)  58 us
    slice x8, local copies, waits for them, and re-layouts, pedigree_inverse(): back[:, lag * block_len:(lag + 1) * block_len]  36 us
    psum x2, blocking collectives, body(): marker_sums = lax.psum(partial_sums, 'snp')  28.3 us
  transfers between devices with their start and end apart: 14, of which 2 were waited for; matrix products, arithmetic and copies ran while one was open for 57% of the time, Pallas kernels for 0%

commit v1 on v0

v1 whole, which is shorter than its diff:
```python
import functools
import types

import jax
import jax.numpy as jnp
from jax import lax
from jax.experimental import pallas as pl
from jax.experimental.pallas import tpu as pltpu
from jax.sharding import PartitionSpec as P

SPAN = 3
ITERS = 2
TRAITS = 4
HI = 256
OWN = 256
F32 = jnp.float32
BF16 = jnp.bfloat16
MESH = pl.DeviceIdType.MESH


def split(x):
    high = x.astype(BF16)
    return high, (x - high.astype(F32)).astype(BF16)


def mix(matrix, field):
    total = matrix[:, 0:1] * field[0:1, :]
    for u in range(1, TRAITS):
        total = total + matrix[:, u : u + 1] * field[u : u + 1, :]
    return total


def fold(x):
    total = x[:, 0:128]
    for i in range(1, x.shape[1] // 128):
        total = total + x[:, i * 128 : (i + 1) * 128]
    return jnp.sum(total, axis=0, keepdims=True)


def total_of(row):
    return jnp.sum(row, axis=1, keepdims=True)


def kernel(nc, nz, inputs, names, *refs):
    r = types.SimpleNamespace(**dict(zip(names, refs)))
    c = lax.axis_index("cohort")
    z = lax.axis_index("snp")
    slots = r.rhs_a.shape[1]
    part = slots // nz
    lows = slots // HI
    rows = lows * TRAITS
    prow = rows // nz
    snps = r.rhs_s.shape[1]
    genos = r.geno_idx.shape[1]
    owners = snps // OWN
    chunk = r.geno_f32.shape[2]
    chunks = snps // chunk
    own = lax.rem(c, owners)
    is_owner = c < owners
    own_at = pl.ds(pl.multiple_of(own * OWN, OWN), OWN)
    my_slots = pl.ds(pl.multiple_of(z * part, part), part)
    my_rows = pl.ds(pl.multiple_of(z * prow, prow), prow)

    def cohort_at(k):
        return lax.rem(c + k + nc, nc)

    def send(src, dst, send_sem, recv_sem, device):
        pltpu.make_async_remote_copy(
            src_ref=src, dst_ref=dst, send_sem=send_sem, recv_sem=recv_sem,
            device_id=device, device_id_type=MESH,
        ).start()

    def wait(ref, sem):
        pltpu.make_async_copy(ref, ref, sem).wait()

    loads = []
    for i, name in enumerate(inputs):
        loads.append(pltpu.make_async_copy(getattr(r, "in_" + name), getattr(r, name), r.load_sem.at[i]))
    for j in range(chunks):
        loads.append(
            pltpu.make_async_copy(
                r.in_genotypes.at[:, j * chunk : (j + 1) * chunk],
                r.geno_f32.at[j],
                r.load_sem.at[len(inputs) + j],
            )
        )
    for load in loads:
        load.start()

    barrier = pltpu.get_barrier_semaphore()

    @pl.loop(1, nz)
    def _(k):
        pl.semaphore_signal(barrier, inc=1, device_id=(c, lax.rem(z + k, nz)), device_id_type=MESH)

    @pl.loop(1, nc)
    def _(k):
        pl.semaphore_signal(barrier, inc=1, device_id=(cohort_at(k), z), device_id_type=MESH)

    for load in loads[: len(inputs)]:
        load.wait()

    r.idx_own[0:1, :] = r.sire[:, my_slots]
    r.idx_own[1:2, :] = r.dam[:, my_slots]

    pl.semaphore_wait(barrier, nz - 1 + nc - 1)

    for l in range(SPAN):
        send(
            r.idx_own, r.idx_recv.at[l], r.idx_ssem.at[l], r.idx_rsem.at[l],
            (cohort_at(-(l + 1)), z),
        )

    cohort_row = lax.broadcasted_iota(jnp.int32, (1, nc), 1)
    live_count = total_of(jnp.where(cohort_row == c, r.sizes[...].astype(F32), 0.0))

    @pl.loop(0, lows // 2)
    def _(j):
        here = pl.ds(pl.multiple_of(j * 2 * HI, 2 * HI), 2 * HI)
        slot = (lax.broadcasted_iota(jnp.int32, (1, 2 * HI), 1) + j * 2 * HI).astype(F32)
        res = jnp.where(slot < live_count, r.rhs_a[:, here], 0.0)
        r.res_a0[:, here] = res
        pre = r.pre_a[0, :, here] * res[0:1, :]
        for u in range(1, TRAITS):
            pre = pre + r.pre_a[u, :, here] * res[u : u + 1, :]
        r.z_a0[:, here] = pre
        r.field[0, pl.ds(pl.multiple_of(j * 8, 8), 8), :] = jnp.concatenate(
            [pre[:, :HI], pre[:, HI:]], axis=0
        )

    def precond_s(res, at):
        pre = r.pre_s[0, :, at] * res[0:1, :]
        for u in range(1, TRAITS):
            pre = pre + r.pre_s[u, :, at] * res[u : u + 1, :]
        return pre

    def precond_a(res):
        pre = r.pre_a[0, :, my_slots] * res[0:1, :]
        for u in range(1, TRAITS):
            pre = pre + r.pre_a[u, :, my_slots] * res[u : u + 1, :]
        return pre

    def marker_product(step, first):
        r.acc_m[...] = jnp.zeros_like(r.acc_m)
        if first:
            for load in loads[len(inputs) :]:
                load.wait()

        @pl.loop(0, chunks)
        def _(j):
            at = pl.ds(pl.multiple_of(j * chunk, chunk), chunk)
            if first:
                z_s = precond_s(r.rhs_s[:, at], at)
                r.z_s[0, :, at] = z_s
                high, low = split(r.geno_f32[j])
                r.geno_hi[j] = high
                r.geno_lo[j] = low
            else:
                z_s = r.z_s[step, :, at]
                high, low = r.geno_hi[j], r.geno_lo[j]
            s_high, s_low = split(z_s)
            both = jnp.concatenate([s_high.astype(F32), s_low.astype(F32)], axis=0).astype(BF16)
            dims = (((1,), (1,)), ((), ()))
            r.acc_m[...] += lax.dot_general(
                both, high, dims, preferred_element_type=F32
            ) + lax.dot_general(both, low, dims, preferred_element_type=F32)

        r.mk[step, z] = r.acc_m[0:TRAITS, :] + r.acc_m[TRAITS : 2 * TRAITS, :]

    first_animal = c * slots

    def one_hot(index):
        local = index - first_animal
        high = jnp.bitwise_and(local, HI - 1)
        low = jnp.right_shift(local, 8)
        n = index.shape[1]
        hot = (lax.broadcasted_iota(jnp.int32, (HI, n), 0) == high).astype(F32).astype(BF16)
        key = low - jnp.right_shift(lax.broadcasted_iota(jnp.int32, (8, n), 0), 2)
        return hot, key

    def gather(hot, key):
        picked = jnp.dot(r.field_bf[...], hot, preferred_element_type=F32)
        total = jnp.zeros((8, hot.shape[1]), F32)
        for g in range(rows // 8):
            value = picked[g * 8 : g * 8 + 8, :] + picked[rows + g * 8 : rows + g * 8 + 8, :]
            total = total + jnp.where(key == 2 * g, value, 0.0)
        return total[0:TRAITS, :] + total[TRAITS:8, :]

    def scatter(value, hot, key):
        twice = jnp.concatenate([value, value], axis=0)
        high, low = split(twice)
        pieces = []
        for piece in (high.astype(F32), low.astype(F32)):
            for g in range(rows // 8):
                pieces.append(jnp.where(key == 2 * g, piece, 0.0))
        spread = jnp.concatenate(pieces, axis=0).astype(BF16)
        r.acc_b[...] += lax.dot_general(
            spread, hot, (((1,), (1,)), ((), ())), preferred_element_type=F32
        )

    def to_snp(src_of, dst, send_sem, recv_sem):
        @pl.loop(1, nz)
        def _(k):
            other = lax.rem(z + k, nz)
            send(src_of(other), dst, send_sem, recv_sem, (c, other))

    def to_cohort(src, dst, send_sem, recv_sem):
        @pl.loop(1, nc)
        def _(k):
            send(src, dst, send_sem, recv_sem, (cohort_at(k), z))

    row4 = lax.broadcasted_iota(jnp.int32, (4, 128), 0)
    sire, dam = r.idx_own[0:1, :], r.idx_own[1:2, :]
    known = jnp.where(sire >= 0, 1.0, 0.0) + jnp.where(dam >= 0, 1.0, 0.0)
    factor = 4.0 / (4.0 - known)
    gen_inv, res_inv, coup, prior = (x[...] for x in (r.gen_inv, r.res_inv, r.coup, r.prior))
    at_z0 = jnp.where(z == 0, 1.0, 0.0)
    at_owner = jnp.where(is_owner, 1.0, 0.0)
    gamma0 = delta0 = alpha0 = None

    for step in range(ITERS):
        high, low = split(r.field[step])
        r.field_bf[0:rows, :] = high
        r.field_bf[rows : 2 * rows, :] = low

        if step == 0:
            marker_product(0, True)
            to_snp(lambda o: r.mk.at[0, z], r.mk.at[0, z], r.mk_ssem.at[0], r.mk_rsem.at[0])
            hot, key = one_hot(r.geno_idx[...])
            r.hot_g[...] = hot
            r.key_g[...] = key

        @pl.loop(0, SPAN)
        def _(l):
            if step == 0:
                wait(r.idx_recv.at[l], r.idx_rsem.at[l])
                for k in range(2):
                    hot, key = one_hot(r.idx_recv[l, k : k + 1, :])
                    r.hot[2 * l + k] = hot
                    r.key[2 * l + k] = key
            total = gather(r.hot[2 * l], r.key[2 * l])
            r.up_send[step, l] = total + gather(r.hot[2 * l + 1], r.key[2 * l + 1])
            send(
                r.up_send.at[step, l], r.up_recv.at[step, l],
                r.up_ssem.at[step, l], r.up_rsem.at[step, l], (cohort_at(l + 1), z),
            )

        if step > 0:
            @pl.when(is_owner)
            def _():
                wait(r.z_s.at[step, :, pl.ds(0, (owners - 1) * OWN)], r.zs_rsem)

            @pl.when(jnp.logical_not(is_owner))
            def _():
                wait(r.z_s.at[step], r.zs_rsem)

            marker_product(step, False)
            to_snp(
                lambda o: r.mk.at[step, z], r.mk.at[step, z],
                r.mk_ssem.at[step], r.mk_rsem.at[step],
            )
        dir_g = gather(r.hot_g[...], r.key_g[...])
        wait(r.mk.at[step, pl.ds(0, nz - 1)], r.mk_rsem.at[step])
        mismatch = dir_g - jnp.sum(r.mk[step], axis=0)
        tied = mix(coup, mismatch)

        t_high, t_low = split(tied)
        both = jnp.concatenate([t_high.astype(F32), t_low.astype(F32)], axis=0).astype(BF16)

        @pl.loop(0, chunks)
        def _(j):
            at = pl.ds(pl.multiple_of(j * chunk, chunk), chunk)
            sums = jnp.dot(both, r.geno_hi[j], preferred_element_type=F32) + jnp.dot(
                both, r.geno_lo[j], preferred_element_type=F32
            )
            r.part_s[step, :, at] = sums[0:TRAITS, :] + sums[TRAITS : 2 * TRAITS, :]

        r.sum_s[step, c] = r.part_s[step, :, own_at]

        @pl.loop(1, nc)
        def _(k):
            other = cohort_at(k)

            @pl.when(other < owners)
            def _():
                send(
                    r.part_s.at[step, :, pl.ds(pl.multiple_of(other * OWN, OWN), OWN)],
                    r.sum_s.at[step, c],
                    r.ss_ssem.at[step], r.ss_rsem.at[step], (other, z),
                )

        for l in range(SPAN):
            wait(r.up_recv.at[step, l], r.up_rsem.at[step, l])
        z_own = r.z_a0[:, my_slots] if step == 0 else r.z_own[...]
        parents = r.up_recv[step, 0] + r.up_recv[step, 1] + r.up_recv[step, 2]
        deviation = z_own - 0.5 * parents
        mixed = mix(gen_inv, factor * deviation)
        r.down_send[step] = mixed
        for l in range(SPAN):
            send(
                r.down_send.at[step], r.down_recv.at[step, l],
                r.down_ssem.at[step, l], r.down_rsem.at[step, l], (cohort_at(-(l + 1)), z),
            )
        own_image = r.weight[:, my_slots] * mix(res_inv, z_own)
        zs_own = r.z_s[step, :, own_at]
        prior_image = mix(prior, zs_own)
        curve = (
            fold(z_own * own_image + deviation * mixed)
            + at_z0 * fold(mismatch * tied)
            + at_owner * fold(zs_own * prior_image)
        )
        if step == 0:
            gamma_row = fold(z_own * r.res_a0[:, my_slots]) + at_owner * fold(
                zs_own * r.rhs_s[:, own_at]
            )
            cross_row = jnp.zeros((1, 128), F32)
        else:
            gamma_row, cross_row = gamma1_row, cross1_row
        r.dot_z[step, z] = jnp.where(
            row4 == 0, gamma_row, jnp.where(row4 == 1, curve, jnp.where(row4 == 2, cross_row, 0.0))
        )
        to_snp(
            lambda o: r.dot_z.at[step, z], r.dot_z.at[step, z],
            r.dz_ssem.at[step], r.dz_rsem.at[step],
        )

        r.acc_b[...] = jnp.zeros_like(r.acc_b)
        scatter(at_z0 * tied, r.hot_g[...], r.key_g[...])
        wait(r.dot_z.at[step, pl.ds(0, nz - 1)], r.dz_rsem.at[step])
        r.dot_c[step, c] = jnp.sum(r.dot_z[step], axis=0)
        to_cohort(
            r.dot_c.at[step, c], r.dot_c.at[step, c],
            r.dc_ssem.at[step], r.dc_rsem.at[step],
        )

        @pl.loop(0, SPAN)
        def _(l):
            wait(r.down_recv.at[step, l], r.down_rsem.at[step, l])
            value = -0.5 * r.down_recv[step, l]
            scatter(value, r.hot[2 * l], r.key[2 * l])
            scatter(value, r.hot[2 * l + 1], r.key[2 * l + 1])

        r.back[step] = r.acc_b[0:rows, :] + r.acc_b[rows : 2 * rows, :]
        r.back_recv[step, z] = r.back[step, my_rows, :]
        to_snp(
            lambda o: r.back.at[step, pl.ds(pl.multiple_of(o * prow, prow), prow), :],
            r.back_recv.at[step, z], r.bk_ssem.at[step], r.bk_rsem.at[step],
        )

        wait(r.dot_c.at[step, pl.ds(0, nc - 1)], r.dc_rsem.at[step])
        dots = jnp.sum(r.dot_c[step], axis=0)
        if step == 0:
            gamma0, delta0 = total_of(dots[0:1, :]), total_of(dots[1:2, :])
            alpha = alpha0 = gamma0 / delta0
            beta = None
        else:
            gamma1, delta_z, cross = (total_of(dots[i : i + 1, :]) for i in range(3))
            beta = gamma1 / gamma0
            alpha = gamma1 / (delta_z + 2.0 * beta * cross + beta * beta * delta0)

        @pl.when(is_owner)
        def _():
            wait(r.sum_s.at[step, pl.ds(0, nc - 1)], r.ss_rsem.at[step])

        image_s = prior_image - jnp.sum(jnp.where(is_owner, r.sum_s[step], 0.0), axis=0)
        if step == 0:
            res_s = r.rhs_s[:, own_at] - alpha * image_s
            r.image_s[...] = image_s
            r.res_s1[...] = res_s
            z_s = precond_s(res_s, own_at)
            target = r.z_s.at[1]
            sems = r.zs_ssem, r.zs_rsem
        else:
            z_s = r.res_s1[...] - alpha * (image_s + beta * r.image_s[...])
            target = r.rs_all
            sems = r.rs_ssem, r.rs_rsem

        @pl.when(is_owner)
        def _():
            target[:, own_at] = z_s
            to_cohort(target.at[:, own_at], target.at[:, own_at], *sems)

        if step == 0:
            gamma1_row = at_owner * fold(z_s * res_s)
            cross1_row = at_owner * fold(z_s * image_s)

        wait(r.back_recv.at[step, pl.ds(0, nz - 1)], r.bk_rsem.at[step])
        back = jnp.sum(r.back_recv[step], axis=0)
        back = jnp.concatenate([back[i : i + TRAITS, :] for i in range(0, prow, TRAITS)], axis=1)
        image_a = own_image + mixed + back
        if step == 0:
            res_a = r.res_a0[:, my_slots] - alpha * image_a
            z_a = precond_a(res_a)
            r.image_a[...] = image_a
            r.res_a1[...] = res_a
            r.z_own[...] = z_a
            for i in range(0, prow, 8):
                lo = i // TRAITS
                at = pl.ds(pl.multiple_of(z * prow + i, 8), 8)
                r.field[1, at, :] = jnp.concatenate(
                    [z_a[:, lo * HI : (lo + 1) * HI], z_a[:, (lo + 1) * HI : (lo + 2) * HI]], axis=0
                )
            mine = r.field.at[1, my_rows, :]
            to_snp(lambda o: mine, mine, r.fl_ssem, r.fl_rsem)
            gamma1_row = gamma1_row + fold(z_a * res_a)
            cross1_row = cross1_row + fold(z_a * image_a)
            wait(r.field.at[1, pl.ds(0, rows - prow), :], r.fl_rsem)
        else:
            r.ra_all[:, my_slots] = r.res_a1[...] - alpha * (image_a + beta * r.image_a[...])
            mine = r.ra_all.at[:, my_slots]
            to_snp(lambda o: mine, mine, r.ra_ssem, r.ra_rsem)

    start_part = alpha0 + alpha * beta

    @pl.loop(0, lows // 2)
    def _(j):
        here = pl.ds(pl.multiple_of(j * 2 * HI, 2 * HI), 2 * HI)
        z1 = r.field[1, pl.ds(pl.multiple_of(j * 8, 8), 8), :]
        z1 = jnp.concatenate([z1[0:TRAITS, :], z1[TRAITS:8, :]], axis=1)
        r.sol_a[:, here] = start_part * r.z_a0[:, here] + alpha * z1

    @pl.loop(0, owners)
    def _(j):
        here = pl.ds(pl.multiple_of(j * OWN, OWN), OWN)
        r.sol_s[:, here] = start_part * r.z_s[0, :, here] + alpha * r.z_s[1, :, here]

    @pl.when(is_owner)
    def _():
        wait(r.rs_all.at[:, pl.ds(0, (owners - 1) * OWN)], r.rs_rsem)

    @pl.when(jnp.logical_not(is_owner))
    def _():
        wait(r.rs_all, r.rs_rsem)

    r.out_rs[...] = r.rs_all[...]
    wait(r.ra_all.at[:, pl.ds(0, slots - part)], r.ra_rsem)
    r.out_ra[...] = r.ra_all[...]

    for l in range(SPAN):
        wait(r.idx_own, r.idx_ssem.at[l])
    for step in range(ITERS):
        for l in range(SPAN):
            wait(r.up_send.at[step, l], r.up_ssem.at[step, l])
            wait(r.down_send.at[step], r.down_ssem.at[step, l])
        wait(r.mk.at[step, pl.ds(0, nz - 1)], r.mk_ssem.at[step])
        wait(r.dot_z.at[step, pl.ds(0, nz - 1)], r.dz_ssem.at[step])
        wait(r.dot_c.at[step, pl.ds(0, nc - 1)], r.dc_ssem.at[step])
        wait(r.back_recv.at[step, pl.ds(0, nz - 1)], r.bk_ssem.at[step])

        @pl.when(is_owner)
        def _():
            wait(r.part_s.at[step, :, pl.ds(0, (owners - 1) * OWN)], r.ss_ssem.at[step])

        @pl.when(jnp.logical_not(is_owner))
        def _():
            wait(r.part_s.at[step], r.ss_ssem.at[step])

    @pl.when(is_owner)
    def _():
        wait(r.sum_s.at[0, pl.ds(0, nc - 1)], r.zs_ssem)
        wait(r.sum_s.at[1, pl.ds(0, nc - 1)], r.rs_ssem)

    wait(r.field.at[1, pl.ds(0, rows - prow), :], r.fl_ssem)
    wait(r.ra_all.at[:, pl.ds(0, slots - part)], r.ra_ssem)


def body(nc, nz, rhs_a, rhs_s, weight, sire, dam, sizes, geno_idx, genotypes, pre_a, pre_s, *small):
    slots, snps, genos = rhs_a.shape[1], rhs_s.shape[1], geno_idx.shape[0]
    part = slots // nz
    rows = slots // HI * TRAITS
    chunk = next(k for k in (1280, 1024, 512, 256) if snps % k == 0)
    chunks = snps // chunk
    vmem, dma = pltpu.VMEM, pltpu.SemaphoreType.DMA
    inputs = dict(
        rhs_a=rhs_a, rhs_s=rhs_s, weight=weight[None], sire=sire[None], dam=dam[None], sizes=sizes[None],
        geno_idx=geno_idx[None], pre_a=pre_a, pre_s=pre_s,
        gen_inv=small[0], res_inv=small[1], coup=small[2], prior=small[3],
    )
    scratch = {name: vmem(x.shape, x.dtype) for name, x in inputs.items()}
    scratch |= dict(
        geno_f32=vmem((chunks, genos, chunk), F32),
        geno_hi=vmem((chunks, genos, chunk), BF16),
        geno_lo=vmem((chunks, genos, chunk), BF16),
        idx_own=vmem((2, part), jnp.int32),
        idx_recv=vmem((SPAN, 2, part), jnp.int32),
        hot=vmem((2 * SPAN, HI, part), BF16),
        key=vmem((2 * SPAN, 8, part), jnp.int32),
        hot_g=vmem((HI, genos), BF16),
        key_g=vmem((8, genos), jnp.int32),
        res_a0=vmem((TRAITS, slots), F32),
        z_a0=vmem((TRAITS, slots), F32),
        field=vmem((ITERS, rows, HI), F32),
        field_bf=vmem((2 * rows, HI), BF16),
        z_s=vmem((ITERS, TRAITS, snps), F32),
        acc_m=vmem((2 * TRAITS, genos), F32),
        mk=vmem((ITERS, nz, TRAITS, genos), F32),
        part_s=vmem((ITERS, TRAITS, snps), F32),
        sum_s=vmem((ITERS, nc, TRAITS, OWN), F32),
        up_send=vmem((ITERS, SPAN, TRAITS, part), F32),
        up_recv=vmem((ITERS, SPAN, TRAITS, part), F32),
        down_send=vmem((ITERS, TRAITS, part), F32),
        down_recv=vmem((ITERS, SPAN, TRAITS, part), F32),
        dot_z=vmem((ITERS, nz, 4, 128), F32),
        dot_c=vmem((ITERS, nc, 4, 128), F32),
        acc_b=vmem((2 * rows, HI), F32),
        back=vmem((ITERS, rows, HI), F32),
        back_recv=vmem((ITERS, nz, rows // nz, HI), F32),
        image_a=vmem((TRAITS, part), F32),
        res_a1=vmem((TRAITS, part), F32),
        z_own=vmem((TRAITS, part), F32),
        image_s=vmem((TRAITS, OWN), F32),
        res_s1=vmem((TRAITS, OWN), F32),
        ra_all=vmem((TRAITS, slots), F32),
        rs_all=vmem((TRAITS, snps), F32),
        load_sem=dma((len(inputs) + chunks,)),
    )
    for name, shape in dict(
        idx=(SPAN,), up=(ITERS, SPAN), down=(ITERS, SPAN), mk=(ITERS,), ss=(ITERS,), dz=(ITERS,), dc=(ITERS,),
        bk=(ITERS,), zs=(), rs=(), fl=(), ra=(),
    ).items():
        scratch[name + "_ssem"] = dma(shape)
        scratch[name + "_rsem"] = dma(shape)
    names = ["in_" + name for name in inputs] + ["in_genotypes"]
    names += ["sol_a", "sol_s", "out_ra", "out_rs"] + list(scratch)
    outs = [jax.ShapeDtypeStruct(x.shape, F32) for x in (rhs_a, rhs_s, rhs_a, rhs_s)]
    return pl.pallas_call(
        functools.partial(kernel, nc, nz, list(inputs), names),
        out_shape=outs,
        in_specs=[pl.BlockSpec(memory_space=pl.ANY)] * (len(inputs) + 1),
        out_specs=[pl.BlockSpec(memory_space=pltpu.VMEM)] * 4,
        scratch_shapes=list(scratch.values()),
        compiler_params=pltpu.CompilerParams(
            collective_id=0, has_side_effects=True, vmem_limit_bytes=48 * 1024 * 1024
        ),
        cost_estimate=pl.CostEstimate(flops=4 * 10**9, bytes_accessed=10**7, transcendentals=0),
    )(*inputs.values(), genotypes)


def solution(mesh):
    nc, nz = mesh.shape["cohort"], mesh.shape["snp"]
    in_specs = (
        P(None, "cohort"),
        P(None, "snp"),
        P("cohort"),
        P("cohort"),
        P("cohort"),
        P(),
        P("cohort"),
        P("cohort", "snp"),
        P(None, None, "cohort"),
        P(None, None, "snp"),
        P(),
        P(),
        P(),
        P(),
    )
    out_specs = (P(None, "cohort"), P(None, "snp"), P(None, "cohort"), P(None, "snp"))
    return jax.shard_map(
        functools.partial(body, nc, nz), mesh=mesh, in_specs=in_specs, out_specs=out_specs, check_vma=False
    )
```

time: 879 us -> 80.7 us (0.09)
  the two profiles are of different devices: /device:TPU:1 before, /device:TPU:32 now
where the time goes in v1:
time: 80.7 us; the launch traced here: 80.2 us
  Pallas kernels  66.8 us (83%)
  local copies, waits for them, and re-layouts  12.8 us (16%)
    pallas_call x1, Pallas kernels, body(): pl.pallas_call(functools.partial(kernel, nc, nz, list(inputs), names), ou...  66.8 us
    unnamed x30, local copies, waits for them, and re-layouts  12.8 us

profile of v1, /device:TPU:32, one launch (start us, length us, event | category | flops | bytes accessed | tf_op | source)
XLA Modules:
  0.0 80.2 jit_solution(9232914808286148340)
XLA Ops:
  0.6 0.0 copy-start
  0.6 1.0 %copy-done = f32[4,4,8192]{2,1,0:T(4,128)S(1)} copy-done((f32[4,4,8192]{2,1,0:T(4,128)S(1)}, f32[4,4,8192]{2,1,0:T(4,128)}, u32[]{:S(2)}) %copy-start) | copy-done | bytes 524312
  1.7 0.0 copy-start.1
  1.7 1.0 %copy-done.1 = f32[4,4,6400]{2,1,0:T(4,128)S(1)} copy-done((f32[4,4,6400]{2,1,0:T(4,128)S(1)}, f32[4,4,6400]{2,1,0:T(4,128)}, u32[]{:S(2)}) %copy-start.1) | copy-done | bytes 409624
  2.7 0.0 copy-start.2
  2.7 0.9 %copy-done.2 = f32[4,8192]{1,0:T(4,128)S(1)} copy-done((f32[4,8192]{1,0:T(4,128)S(1)}, f32[4,8192]{1,0:T(4,128)}, u32[]{:S(2)}) %copy-start.2) | copy-done | bytes 131096
  3.6 0.0 copy-start.3
  3.6 0.9 %copy-done.3 = f32[4,6400]{1,0:T(4,128)S(1)} copy-done((f32[4,6400]{1,0:T(4,128)S(1)}, f32[4,6400]{1,0:T(4,128)}, u32[]{:S(2)}) %copy-start.3) | copy-done | bytes 102424
  4.5 0.0 copy-start.4
  4.5 0.8 copy-done.4
  5.2 0.0 copy-start.5
  5.2 0.8 copy-done.5
  6.0 0.0 copy-start.6
  6.0 0.8 copy-done.6
  6.8 0.0 copy-start.7
  6.8 0.7 copy-done.7
  7.4 0.0 copy-start.8
  7.4 0.7 copy-done.8
  8.1 0.0 copy-start.9
  8.1 0.7 copy-done.9
  8.8 0.0 copy-start.10
  8.8 0.7 copy-done.10
  9.5 0.0 copy-start.11
  9.5 0.7 copy-done.11
  10.2 0.0 copy-start.12
  10.2 0.7 copy-done.12
  10.8 66.8 %shard_map.165 = (f32[4,8192]{1,0:T(4,128)S(1)}, f32[4,6400]{1,0:T(4,128)S(1)}, f32[4,8192]{1,0:T(4,128)S(1)}, f32[4,6400]{1,0:T(4,128)S(1)}) custom-call(f32[4,8192]{1,0:T(4,128)S(1)} %copy-done.2, f32[4,6400]{1,0:T(4,128)S(1)} %copy-done.3, f32[1,8192]{1,0:T(1,128)S(1)} %bitcast.5, s32[1,8192]{1,0:T(1,128)S(1)} %bitcast.6, s32[1,8192]{1,0:T(1,128)S(1)} %bitcast.7, ...), custom_call_target="tpu_custom_call" | custom-call | flops 4000000000 | bytes 10000000 | tf_op jit(solution)/shard_map/pallas_call | solution.py:526
  77.6 0.7 copy.22
  78.2 0.6 copy.23
  78.9 0.7 copy.24
  79.5 0.6 copy.25
Async XLA Ops:
  0.6 1.0 %copy-start = (f32[4,4,8192]{2,1,0:T(4,128)S(1)}, f32[4,4,8192]{2,1,0:T(4,128)}, u32[]{:S(2)}) copy-start(f32[4,4,8192]{2,1,0:T(4,128)} %refs_7_.1) | copy-start | bytes 1572868
  1.7 1.0 %copy-start.1 = (f32[4,4,6400]{2,1,0:T(4,128)S(1)}, f32[4,4,6400]{2,1,0:T(4,128)}, u32[]{:S(2)}) copy-start(f32[4,4,6400]{2,1,0:T(4,128)} %refs_8_.1) | copy-start | bytes 1228804
  2.7 0.9 %copy-start.2 = (f32[4,8192]{1,0:T(4,128)S(1)}, f32[4,8192]{1,0:T(4,128)}, u32[]{:S(2)}) copy-start(f32[4,8192]{1,0:T(4,128)} %refs_0_.1) | copy-start | bytes 393220
  3.6 0.9 %copy-start.3 = (f32[4,6400]{1,0:T(4,128)S(1)}, f32[4,6400]{1,0:T(4,128)}, u32[]{:S(2)}) copy-start(f32[4,6400]{1,0:T(4,128)} %refs_1_.1) | copy-start | bytes 307204
  4.5 0.8 copy-start.4
  5.2 0.8 copy-start.5
  6.0 0.8 copy-start.6
  6.8 0.7 copy-start.7
  7.4 0.7 copy-start.8
  8.1 0.7 copy-start.9
  8.8 0.7 copy-start.10
  9.5 0.7 copy-start.11
  10.2 0.7 copy-start.12

commit v2 on v1

v2 whole, which is shorter than its diff:
```python
import functools
import types

import jax
import jax.numpy as jnp
from jax import lax
from jax.experimental import pallas as pl
from jax.experimental.pallas import tpu as pltpu
from jax.sharding import PartitionSpec as P

SPAN = 3
TRAITS = 4
HI = 256
OWN = 256
F32 = jnp.float32
BF16 = jnp.bfloat16
MESH = pl.DeviceIdType.MESH


def split(x):
    high = x.astype(BF16)
    return high, (x - high.astype(F32)).astype(BF16)


def stacked_split(x):
    high, low = split(x)
    return jnp.concatenate([high.astype(F32), low.astype(F32)], axis=0).astype(BF16)


def mix(matrix, field):
    total = matrix[:, 0:1] * field[0:1, :]
    for u in range(1, TRAITS):
        total = total + matrix[:, u : u + 1] * field[u : u + 1, :]
    return total


def fold(x):
    total = x[:, 0:128]
    for i in range(1, x.shape[1] // 128):
        total = total + x[:, i * 128 : (i + 1) * 128]
    return jnp.sum(total, axis=0, keepdims=True)


def total_of(row):
    return jnp.sum(row, axis=1, keepdims=True)


def z_plan(nz):
    order = sorted(range(1, nz), key=lambda k: -min(k, nz - k))
    reach = nz // 4
    return order, reach, 2 * reach + 1 if nz >= 4 else nz


def kernel(nc, nz, names, *refs):
    r = types.SimpleNamespace(**dict(zip(names, refs)))
    c = lax.axis_index("cohort")
    z = lax.axis_index("snp")
    slots = r.rhs_a.shape[1]
    part = slots // nz
    lows = slots // HI
    rows = lows * TRAITS
    prow = rows // nz
    snps = r.rhs_s.shape[1]
    owners = snps // OWN
    chunk = r.geno_f32.shape[2]
    chunks = snps // chunk
    own_block = lax.rem(c, owners)
    is_owner = c < owners
    own_at = pl.ds(pl.multiple_of(own_block * OWN, OWN), OWN)
    my_slots = pl.ds(pl.multiple_of(z * part, part), part)
    order, reach, nears = z_plan(nz)
    near_rows = nears * prow
    far_rows = rows - near_rows
    my_rows = slice(reach * prow, (reach + 1) * prow)

    def cohort_at(k):
        return lax.rem(c + k + nc, nc)

    def send(src, dst, send_sem, recv_sem, device):
        pltpu.make_async_remote_copy(
            src_ref=src, dst_ref=dst, send_sem=send_sem, recv_sem=recv_sem,
            device_id=device, device_id_type=MESH,
        ).start()

    def wait(ref, sem):
        pltpu.make_async_copy(ref, ref, sem).wait()

    loads = []
    for src, dst in (
        (r.in_rhs_a, r.rhs_a),
        (r.in_pre_a, r.pre_a),
        (r.in_sizes, r.sizes),
        (r.in_geno_idx, r.geno_idx),
        (r.in_rhs_s, r.rhs_s),
        (r.in_pre_s, r.pre_s),
        (r.in_sire.at[:, my_slots], r.idx_own.at[0]),
        (r.in_dam.at[:, my_slots], r.idx_own.at[1]),
        (r.in_weight.at[:, my_slots], r.weight),
        (r.in_gen_inv, r.gen_inv),
        (r.in_res_inv, r.res_inv),
        (r.in_coup, r.coup),
        (r.in_prior, r.prior),
    ):
        loads.append(pltpu.make_async_copy(src, dst, r.load_sem.at[len(loads)]))
    for j in range(chunks):
        loads.append(
            pltpu.make_async_copy(
                r.in_genotypes.at[:, j * chunk : (j + 1) * chunk], r.geno_f32.at[j], r.load_sem.at[len(loads)]
            )
        )
    for load in loads:
        load.start()

    barrier = pltpu.get_barrier_semaphore()

    @pl.loop(1, nz)
    def _(k):
        pl.semaphore_signal(barrier, inc=1, device_id=(c, lax.rem(z + k, nz)), device_id_type=MESH)

    @pl.loop(1, nc)
    def _(k):
        pl.semaphore_signal(barrier, inc=1, device_id=(cohort_at(k), z), device_id_type=MESH)

    pl.semaphore_wait(barrier, nz - 1 + nc - 1)

    for l in range(SPAN):
        for k, src in enumerate((r.in_sire, r.in_dam)):
            send(
                src.at[:, my_slots], r.idx_recv.at[l, k], r.idx_ssem.at[l], r.idx_rsem.at[l],
                (cohort_at(-(l + 1)), z),
            )

    def to_snp(src_of, dst_of, send_sem, recv_sem_of, ks):
        for k in ks:
            send(src_of(k), dst_of(k), send_sem, recv_sem_of(k), (c, lax.rem(z + k, nz)))

    def around(act):
        ny = min(4, nc // 2)
        nx = nc // (2 * ny)
        x, y, core = c // (2 * ny), c // 2 % ny, c % 2

        @pl.loop(0, nc)
        def _(t):
            to_x = lax.rem(x + t // (2 * ny) + nx // 2, nx)
            to_y = lax.rem(y + t // 2 % ny + ny // 2, ny)
            other = (to_x * ny + to_y) * 2 + lax.rem(core + t, 2)
            pl.when(other != c)(lambda: act(other))

    def to_cohort(src, dst, send_sem, recv_sem):
        around(lambda other: send(src, dst, send_sem, recv_sem, (other, z)))

    for load in loads[:3]:
        load.wait()

    cohort_row = lax.broadcasted_iota(jnp.int32, (1, nc), 1)
    live_count = total_of(jnp.where(cohort_row == c, r.sizes[...].astype(F32), 0.0))

    def place_of(j):
        at = lax.rem(j + lows // 2 - z * (prow // 8) + reach * (prow // 8), lows // 2)
        return pl.ds(pl.multiple_of(at * 8, 8), 8)

    @pl.loop(0, lows // 2)
    def _(j):
        here = pl.ds(pl.multiple_of(j * 2 * HI, 2 * HI), 2 * HI)
        slot = (lax.broadcasted_iota(jnp.int32, (1, 2 * HI), 1) + j * 2 * HI).astype(F32)
        res = jnp.where(slot < live_count, r.rhs_a[:, here], 0.0)
        r.res_a0[:, here] = res
        pre = r.pre_a[0, :, here] * res[0:1, :]
        for u in range(1, TRAITS):
            pre = pre + r.pre_a[u, :, here] * res[u : u + 1, :]
        r.z_a0[:, here] = pre
        r.field[0, place_of(j), :] = jnp.concatenate([pre[:, :HI], pre[:, HI:]], axis=0)

    def precond_s(res, at):
        pre = r.pre_s[0, :, at] * res[0:1, :]
        for u in range(1, TRAITS):
            pre = pre + r.pre_s[u, :, at] * res[u : u + 1, :]
        return pre

    def precond_a(res):
        pre = r.pre_a[0, :, my_slots] * res[0:1, :]
        for u in range(1, TRAITS):
            pre = pre + r.pre_a[u, :, my_slots] * res[u : u + 1, :]
        return pre

    def marker_product(step):
        r.acc_m[...] = jnp.zeros_like(r.acc_m)

        @pl.loop(0, chunks)
        def _(j):
            at = pl.ds(pl.multiple_of(j * chunk, chunk), chunk)
            if step == 0:
                z_s = precond_s(r.rhs_s[:, at], at)
                r.z_s[0, :, at] = z_s
                high, low = split(r.geno_f32[j])
                r.geno_hi[j] = high
                r.geno_lo[j] = low
            else:
                z_s = r.z_s[step, :, at]
                high, low = r.geno_hi[j], r.geno_lo[j]
            both = stacked_split(z_s)
            dims = (((1,), (1,)), ((), ()))
            r.acc_m[...] += lax.dot_general(
                both, high, dims, preferred_element_type=F32
            ) + lax.dot_general(both, low, dims, preferred_element_type=F32)

        r.mk[step, z] = r.acc_m[0:TRAITS, :] + r.acc_m[TRAITS : 2 * TRAITS, :]
        mine = r.mk.at[step, z]
        to_snp(lambda k: mine, lambda k: mine, r.mk_ssem.at[step], lambda k: r.mk_rsem.at[step], order)

    first_animal = c * slots

    def one_hot(index):
        local = index - first_animal
        high = jnp.bitwise_and(local, HI - 1)
        low = jnp.right_shift(local, 8)
        n = index.shape[1]
        hot = (lax.broadcasted_iota(jnp.int32, (HI, n), 0) == high).astype(F32).astype(BF16)
        here = jnp.logical_and(low >= 0, low < lows)
        around_low = jnp.bitwise_and(low + (reach - z) * (lows // nz), lows - 1)
        place = jnp.where(here, around_low, -8)
        return hot, place - jnp.right_shift(lax.broadcasted_iota(jnp.int32, (8, n), 0), 2)

    near_part, far_part = (0, near_rows), (near_rows, far_rows)

    def load_field(step, which):
        first, count = which
        high, low = split(r.field[step, first : first + count, :])
        r.field_bf[2 * first : 2 * first + count, :] = high
        r.field_bf[2 * first + count : 2 * (first + count), :] = low

    def gather(which, hot, key):
        first, count = which
        picked = jnp.dot(
            r.field_bf[2 * first : 2 * (first + count), :], hot, preferred_element_type=F32
        )
        total = jnp.zeros((8, hot.shape[1]), F32)
        for g in range(count // 8):
            value = picked[g * 8 : g * 8 + 8, :] + picked[count + g * 8 : count + g * 8 + 8, :]
            total = total + jnp.where(key == 2 * (g + first // 8), value, 0.0)
        return total

    def gather_all(which, l):
        return gather(which, r.hot[2 * l], r.key[2 * l]) + gather(which, r.hot[2 * l + 1], r.key[2 * l + 1])

    def halves(total):
        return total[0:TRAITS, :] + total[TRAITS:8, :]

    def scatter(which, value, hot, key):
        first, count = which
        high, low = split(jnp.concatenate([value, value], axis=0))
        pieces = []
        for piece in (high.astype(F32), low.astype(F32)):
            for g in range(count // 8):
                pieces.append(jnp.where(key == 2 * (g + first // 8), piece, 0.0))
        spread = jnp.concatenate(pieces, axis=0).astype(BF16)
        return lax.dot_general(spread, hot, (((1,), (1,)), ((), ())), preferred_element_type=F32)

    def slots_of(block):
        return jnp.concatenate([block[i : i + TRAITS, :] for i in range(0, prow, TRAITS)], axis=1)

    readers = (((1, 0), (-1, 6), (-2, 8)), ((1, 1), (2, 3), (-1, 7)), ((1, 2), (2, 4), (3, 5)))

    def send_sums_up(step, l):
        def to(readers_l):
            for offset, place_there in readers_l:
                send(
                    r.up_own.at[step, l], r.up_recv.at[step, place_there],
                    r.up_ssem.at[step], r.up_rsem.at[step], (cohort_at(offset), z),
                )

        for i in range(SPAN):
            pl.when(l == i)(functools.partial(to, readers[i]))

    def send_own(step, src):
        for l in reversed(range(SPAN)):
            send(
                src, r.own_recv.at[step, l], r.own_ssem.at[step], r.own_rsem.at[step], (cohort_at(-(l + 1)), z)
            )

    def factor_of(sire, dam):
        known = jnp.where(sire >= 0, 1.0, 0.0) + jnp.where(dam >= 0, 1.0, 0.0)
        return 4.0 / (4.0 - known)

    row4 = lax.broadcasted_iota(jnp.int32, (4, 128), 0)
    at_owner = jnp.where(is_owner, 1.0, 0.0)
    every = (near_part, far_part) if far_rows else (near_part,)

    send_own(0, r.z_a0.at[:, my_slots])
    for load in loads[3:]:
        load.wait()
    gen_inv, res_inv, coup, prior = (x[...] for x in (r.gen_inv, r.res_inv, r.coup, r.prior))
    factor = factor_of(r.idx_own[0], r.idx_own[1])

    for step in range(2):
        if step == 0:
            marker_product(0)
            for which in every:
                load_field(0, which)

            @pl.loop(0, SPAN)
            def _(i):
                l = SPAN - 1 - i
                wait(r.idx_recv.at[l], r.idx_rsem.at[l])
                for k in range(2):
                    hot, key = one_hot(r.idx_recv[l, k])
                    r.hot[2 * l + k] = hot
                    r.key[2 * l + k] = key
                r.up_own[0, l] = halves(sum(gather_all(which, l) for which in every))
                send_sums_up(0, l)
                r.factor[l] = factor_of(r.idx_recv[l, 0], r.idx_recv[l, 1])

            hot, key = one_hot(r.geno_idx[...])
            r.hot_g[...] = hot
            r.key_g[...] = key
        else:
            if nears > 1:
                wait(r.field.at[1, pl.ds(0, near_rows - prow), :], r.fl_rsem.at[0])
            load_field(1, near_part)

            @pl.loop(0, SPAN)
            def _(l):
                r.partial[l] = gather_all(near_part, l)

            if far_rows:
                wait(r.field.at[1, near_rows:, :], r.fl_rsem.at[1])
                load_field(1, far_part)

            @pl.loop(0, SPAN)
            def _(i):
                l = SPAN - 1 - i
                total = r.partial[l]
                if far_rows:
                    total = total + gather_all(far_part, l)
                r.up_own[1, l] = halves(total)
                send_sums_up(1, l)

            @pl.when(is_owner)
            def _():
                wait(r.z_s.at[1, :, pl.ds(0, (owners - 1) * OWN)], r.zs_rsem)

            @pl.when(jnp.logical_not(is_owner))
            def _():
                wait(r.z_s.at[1], r.zs_rsem)

            marker_product(1)

            to_snp(
                lambda k: r.image_a, lambda k: r.q_a.at[:, my_slots], r.qa_ssem, lambda k: r.qa_rsem, order
            )
            r.q_a[:, my_slots] = r.image_a[...]

        dir_g = halves(sum(gather(which, r.hot_g[...], r.key_g[...]) for which in every))

        wait(r.own_recv.at[step], r.own_rsem.at[step])
        wait(r.up_recv.at[step], r.up_rsem.at[step])
        others = ((1, 4), (2, 6), (7, 8))
        for l in range(SPAN):
            parents = r.up_own[step, l] + r.up_recv[step, others[l][0]] + r.up_recv[step, others[l][1]]
            terms = r.factor[l] * (r.own_recv[step, l] - 0.5 * parents)
            r.terms[l] = -0.5 * mix(gen_inv, terms)
        r.acc_b[...] = jnp.zeros_like(r.acc_b)

        @pl.loop(0, SPAN)
        def _(l):
            r.acc_b[...] += scatter((0, rows), r.terms[l], r.hot[2 * l], r.key[2 * l]) + scatter(
                (0, rows), r.terms[l], r.hot[2 * l + 1], r.key[2 * l + 1]
            )

        r.back[step] = r.acc_b[0:rows, :] + r.acc_b[rows : 2 * rows, :]
        to_snp(
            lambda k: r.back.at[step, pl.ds((k + reach) % nz * prow, prow), :],
            lambda k: r.back_recv.at[step, k], r.bk_ssem.at[step], lambda k: r.bk_rsem.at[step], order,
        )
        r.back_recv[step, 0] = r.back[step, my_rows, :]

        own = r.z_a0[:, my_slots] if step == 0 else r.y_own[...]
        deviation = own - 0.5 * (r.up_recv[step, 0] + r.up_recv[step, 3] + r.up_recv[step, 5])
        mixed = mix(gen_inv, factor * deviation)
        local_a = r.weight[...] * mix(res_inv, own) + mixed
        own_s = r.z_s[step, :, own_at]
        local_s = mix(prior, own_s)
        if step == 0:
            r.local_s[...] = local_s
            r.deviation[...] = deviation
            curve = fold(own * (local_a - mixed) + deviation * mixed) + at_owner * fold(own_s * local_s)
            gamma_row = fold(own * r.res_a0[:, my_slots]) + at_owner * fold(own_s * r.rhs_s[:, own_at])
            cross_row = jnp.zeros((1, 128), F32)
        else:
            wait(r.dot_c.at[0, pl.ds(0, nc - 1)], r.dc_rsem.at[0])
            dots = jnp.sum(r.dot_c[0], axis=0)
            gamma0, delta0 = total_of(dots[0:1, :]), total_of(dots[1:2, :])
            alpha0 = gamma0 / delta0
            z_own = r.z_a0[:, my_slots] - alpha0 * own
            res_a1 = r.res_a0[:, my_slots] - alpha0 * r.image_a[...]
            zs_own = r.z_s[0, :, own_at] - alpha0 * own_s
            res_s1 = r.rhs_s[:, own_at] - alpha0 * r.image_s[...]
            gamma_row = fold(z_own * res_a1) + at_owner * fold(zs_own * res_s1)
            cross_row = fold(z_own * r.image_a[...]) + at_owner * fold(zs_own * r.image_s[...])
            deviation = r.deviation[...] - alpha0 * deviation
            z_mixed = mix(gen_inv, factor * deviation)
            record = r.weight[...] * mix(res_inv, z_own)
            curve = fold(z_own * record + deviation * z_mixed) + at_owner * fold(
                zs_own * (r.local_s[...] - alpha0 * local_s)
            )
        r.dot_z[step, z] = jnp.where(
            row4 == 0, gamma_row, jnp.where(row4 == 1, curve, jnp.where(row4 == 2, cross_row, 0.0))
        )
        my_dots = r.dot_z.at[step, z]
        to_snp(lambda k: my_dots, lambda k: my_dots, r.dz_ssem.at[step], lambda k: r.dz_rsem.at[step], order)

        wait(r.mk.at[step, pl.ds(0, nz - 1)], r.mk_rsem.at[step])
        mismatch = dir_g - jnp.sum(r.mk[step], axis=0)
        tied = mix(coup, mismatch)

        both = stacked_split(tied)

        @pl.loop(0, chunks)
        def _(j):
            at = pl.ds(pl.multiple_of(j * chunk, chunk), chunk)
            sums = jnp.dot(both, r.geno_hi[j], preferred_element_type=F32) + jnp.dot(
                both, r.geno_lo[j], preferred_element_type=F32
            )
            r.part_s[step, :, at] = sums[0:TRAITS, :] + sums[TRAITS : 2 * TRAITS, :]

        r.sum_s[step, c] = r.part_s[step, :, own_at]

        def send_sums(other):
            @pl.when(other < owners)
            def _():
                send(
                    r.part_s.at[step, :, pl.ds(pl.multiple_of(other * OWN, OWN), OWN)],
                    r.sum_s.at[step, c], r.ss_ssem.at[step], r.ss_rsem.at[step], (other, z),
                )

        around(send_sums)

        if step == 0:
            r.mismatch[...] = mismatch
            tied_row = fold(mismatch * tied)
        else:
            mismatch = r.mismatch[...] - alpha0 * mismatch
            tied_row = fold(mismatch * mix(coup, mismatch))
        wait(r.dot_z.at[step, pl.ds(0, nz - 1)], r.dz_rsem.at[step])
        r.dot_c[step, c] = jnp.sum(r.dot_z[step], axis=0) + jnp.where(row4 == 1, tied_row, 0.0)
        my_dots = r.dot_c.at[step, c]
        to_cohort(my_dots, my_dots, r.dc_ssem.at[step], r.dc_rsem.at[step])

        tie = scatter((reach * prow, prow), tied, r.hot_g[...], r.key_g[...])
        local_a = local_a + slots_of(tie[0:prow, :] + tie[prow : 2 * prow, :])
        wait(r.back_recv.at[step, pl.ds(0, nz - 1)], r.bk_rsem.at[step])
        image_a = local_a + slots_of(jnp.sum(r.back_recv[step], axis=0))
        if step == 0:
            y_a = precond_a(image_a)
            for i in range(0, prow, 8):
                lo = i // TRAITS
                at = reach * prow + i
                r.field[1, at : at + 8, :] = jnp.concatenate(
                    [y_a[:, lo * HI : (lo + 1) * HI], y_a[:, (lo + 1) * HI : (lo + 2) * HI]], axis=0
                )
            mine = r.field.at[1, my_rows, :]
            to_snp(
                lambda k: mine, lambda k: r.field.at[1, pl.ds((reach - k) % nz * prow, prow), :],
                r.fl_ssem, lambda k: r.fl_rsem.at[0 if (reach - k) % nz < nears else 1], order,
            )
            r.y_own[...] = y_a
            r.image_a[...] = image_a
            send_own(1, r.y_own)
        else:
            r.w_own[...] = image_a
            landing = r.w_a.at[:, my_slots]
            to_snp(lambda k: r.w_own, lambda k: landing, r.ra_ssem, lambda k: r.ra_rsem, order)
            r.w_a[:, my_slots] = image_a

        @pl.when(is_owner)
        def _():
            wait(r.sum_s.at[step, pl.ds(0, nc - 1)], r.ss_rsem.at[step])

        image_s = local_s - jnp.sum(jnp.where(is_owner, r.sum_s[step], 0.0), axis=0)
        if step == 0:
            r.image_s[...] = image_s
            y_s = precond_s(image_s, own_at)

            @pl.when(is_owner)
            def _():
                r.z_s[1, :, own_at] = y_s
                mine = r.z_s.at[1, :, own_at]
                to_cohort(mine, mine, r.zs_ssem, r.zs_rsem)
        else:

            @pl.when(is_owner)
            def _():
                r.w_s[:, own_at] = image_s
                mine = r.w_s.at[:, own_at]
                to_cohort(mine, mine, r.rs_ssem, r.rs_rsem)
                r.q_s[:, own_at] = r.image_s[...]
                mine = r.q_s.at[:, own_at]
                to_cohort(mine, mine, r.qs_ssem, r.qs_rsem)

    wait(r.dot_c.at[1, pl.ds(0, nc - 1)], r.dc_rsem.at[1])
    dots = jnp.sum(r.dot_c[1], axis=0)
    gamma1, delta_z, cross = (total_of(dots[i : i + 1, :]) for i in range(3))
    beta = gamma1 / gamma0
    alpha1 = gamma1 / (delta_z + 2.0 * beta * cross + beta * beta * delta0)

    once = alpha0 + alpha1 * (1.0 + beta)
    twice = alpha1 * alpha0
    wait(r.q_a.at[:, pl.ds(0, slots - part)], r.qa_rsem)
    wait(r.w_a.at[:, pl.ds(0, slots - part)], r.ra_rsem)

    @pl.loop(0, lows // 2)
    def _(j):
        here = pl.ds(pl.multiple_of(j * 2 * HI, 2 * HI), 2 * HI)
        y = r.field[1, place_of(j), :]
        y = jnp.concatenate([y[0:TRAITS, :], y[TRAITS:8, :]], axis=1)
        r.out_sol_a[:, here] = once * r.z_a0[:, here] - twice * y
        r.out_ra[:, here] = r.res_a0[:, here] - once * r.q_a[:, here] + twice * r.w_a[:, here]

    for full, sem in ((r.q_s, r.qs_rsem), (r.w_s, r.rs_rsem)):

        @pl.when(is_owner)
        def _():
            wait(full.at[:, pl.ds(0, (owners - 1) * OWN)], sem)

        @pl.when(jnp.logical_not(is_owner))
        def _():
            wait(full, sem)

    @pl.loop(0, owners)
    def _(j):
        here = pl.ds(pl.multiple_of(j * OWN, OWN), OWN)
        r.out_sol_s[:, here] = once * r.z_s[0, :, here] - twice * r.z_s[1, :, here]
        r.out_rs[:, here] = r.rhs_s[:, here] - once * r.q_s[:, here] + twice * r.w_s[:, here]

    for l in range(SPAN):
        wait(r.idx_own, r.idx_ssem.at[l])
    for step in range(2):
        wait(r.up_recv.at[step], r.up_ssem.at[step])
        wait(r.own_recv.at[step], r.own_ssem.at[step])
        wait(r.mk.at[step, pl.ds(0, nz - 1)], r.mk_ssem.at[step])
        wait(r.dot_z.at[step, pl.ds(0, nz - 1)], r.dz_ssem.at[step])
        wait(r.dot_c.at[step, pl.ds(0, nc - 1)], r.dc_ssem.at[step])
        wait(r.back_recv.at[step, pl.ds(0, nz - 1)], r.bk_ssem.at[step])

        @pl.when(is_owner)
        def _():
            wait(r.part_s.at[step, :, pl.ds(0, (owners - 1) * OWN)], r.ss_ssem.at[step])

        @pl.when(jnp.logical_not(is_owner))
        def _():
            wait(r.part_s.at[step], r.ss_ssem.at[step])

    @pl.when(is_owner)
    def _():
        for sem in (r.zs_ssem, r.qs_ssem, r.rs_ssem):
            wait(r.sum_s.at[0, pl.ds(0, nc - 1)], sem)

    wait(r.field.at[1, pl.ds(0, rows - prow), :], r.fl_ssem)
    wait(r.q_a.at[:, pl.ds(0, slots - part)], r.qa_ssem)
    wait(r.w_a.at[:, pl.ds(0, slots - part)], r.ra_ssem)


def place(*refs):
    half = len(refs) // 2
    for i in range(half):
        refs[half + i][...] = refs[i][...]


def body(nc, nz, rhs_a, rhs_s, weight, sire, dam, sizes, geno_idx, genotypes, pre_a, pre_s, *small):
    slots, snps, genos = rhs_a.shape[1], rhs_s.shape[1], geno_idx.shape[0]
    part = slots // nz
    rows = slots // HI * TRAITS
    chunk = next(k for k in (1280, 1024, 512, 256) if snps % k == 0)
    chunks = snps // chunk
    vmem, dma = pltpu.VMEM, pltpu.SemaphoreType.DMA
    inputs = dict(
        rhs_a=rhs_a, rhs_s=rhs_s, weight=weight[None], sire=sire[None], dam=dam[None], sizes=sizes[None],
        geno_idx=geno_idx[None], genotypes=genotypes, pre_a=pre_a, pre_s=pre_s,
        gen_inv=small[0], res_inv=small[1], coup=small[2], prior=small[3],
    )
    scratch = dict(
        rhs_a=vmem(rhs_a.shape, F32),
        rhs_s=vmem(rhs_s.shape, F32),
        weight=vmem((1, part), F32),
        sizes=vmem((1, nc), jnp.int32),
        geno_idx=vmem((1, genos), jnp.int32),
        pre_a=vmem(pre_a.shape, F32),
        pre_s=vmem(pre_s.shape, F32),
        gen_inv=vmem((TRAITS, TRAITS), F32),
        res_inv=vmem((TRAITS, TRAITS), F32),
        coup=vmem((TRAITS, TRAITS), F32),
        prior=vmem((TRAITS, TRAITS), F32),
        geno_f32=vmem((chunks, genos, chunk), F32),
        geno_hi=vmem((chunks, genos, chunk), BF16),
        geno_lo=vmem((chunks, genos, chunk), BF16),
        idx_own=vmem((2, 1, part), jnp.int32),
        idx_recv=vmem((SPAN, 2, 1, part), jnp.int32),
        hot=vmem((2 * SPAN, HI, part), BF16),
        key=vmem((2 * SPAN, 8, part), jnp.int32),
        hot_g=vmem((HI, genos), BF16),
        key_g=vmem((8, genos), jnp.int32),
        res_a0=vmem((TRAITS, slots), F32),
        z_a0=vmem((TRAITS, slots), F32),
        field=vmem((2, rows, HI), F32),
        field_bf=vmem((2 * rows, HI), BF16),
        partial=vmem((SPAN, 8, part), F32),
        z_s=vmem((2, TRAITS, snps), F32),
        acc_m=vmem((2 * TRAITS, genos), F32),
        mk=vmem((2, nz, TRAITS, genos), F32),
        part_s=vmem((2, TRAITS, snps), F32),
        sum_s=vmem((2, nc, TRAITS, OWN), F32),
        factor=vmem((SPAN, 1, part), F32),
        up_own=vmem((2, SPAN, TRAITS, part), F32),
        up_recv=vmem((2, 9, TRAITS, part), F32),
        own_recv=vmem((2, SPAN, TRAITS, part), F32),
        terms=vmem((SPAN, TRAITS, part), F32),
        dot_z=vmem((2, nz, 4, 128), F32),
        dot_c=vmem((2, nc, 4, 128), F32),
        acc_b=vmem((2 * rows, HI), F32),
        back=vmem((2, rows, HI), F32),
        back_recv=vmem((2, nz, rows // nz, HI), F32),
        image_a=vmem((TRAITS, part), F32),
        y_own=vmem((TRAITS, part), F32),
        w_own=vmem((TRAITS, part), F32),
        deviation=vmem((TRAITS, part), F32),
        mismatch=vmem((TRAITS, genos), F32),
        local_s=vmem((TRAITS, OWN), F32),
        image_s=vmem((TRAITS, OWN), F32),
        q_a=vmem((TRAITS, slots), F32),
        w_a=vmem((TRAITS, slots), F32),
        q_s=vmem((TRAITS, snps), F32),
        w_s=vmem((TRAITS, snps), F32),
        load_sem=dma((13 + chunks,)),
    )
    for name, shape in dict(
        idx=(SPAN,), up=(2,), own=(2,), mk=(2,), ss=(2,), dz=(2,), dc=(2,), bk=(2,), zs=(), rs=(), qs=(), qa=(), ra=(),
    ).items():
        scratch[name + "_ssem"] = dma(shape)
        scratch[name + "_rsem"] = dma(shape)
    scratch |= dict(fl_ssem=dma(()), fl_rsem=dma((2,)))
    names = ["in_" + name for name in inputs]
    names += ["out_sol_a", "out_sol_s", "out_ra", "out_rs"] + list(scratch)
    outs = [jax.ShapeDtypeStruct(x.shape, F32) for x in (rhs_a, rhs_s, rhs_a, rhs_s)]
    limit = 56 * 1024 * 1024
    results = pl.pallas_call(
        functools.partial(kernel, nc, nz, names),
        out_shape=outs,
        in_specs=[pl.BlockSpec(memory_space=pl.ANY)] * len(inputs),
        out_specs=[pl.BlockSpec(memory_space=pltpu.VMEM)] * 4,
        scratch_shapes=list(scratch.values()),
        compiler_params=pltpu.CompilerParams(collective_id=0, has_side_effects=True, vmem_limit_bytes=limit),
        cost_estimate=pl.CostEstimate(flops=4 * 10**9, bytes_accessed=10**7, transcendentals=0),
    )(*inputs.values())
    return pl.pallas_call(
        place,
        out_shape=outs,
        in_specs=[pl.BlockSpec(memory_space=pltpu.VMEM)] * 4,
        out_specs=[pl.BlockSpec(memory_space=pltpu.VMEM)] * 4,
    )(*results)


def solution(mesh):
    nc, nz = mesh.shape["cohort"], mesh.shape["snp"]
    in_specs = (
        P(None, "cohort"),
        P(None, "snp"),
        P("cohort"),
        P("cohort"),
        P("cohort"),
        P(),
        P("cohort"),
        P("cohort", "snp"),
        P(None, None, "cohort"),
        P(None, None, "snp"),
        P(),
        P(),
        P(),
        P(),
    )
    out_specs = (P(None, "cohort"), P(None, "snp"), P(None, "cohort"), P(None, "snp"))
    return jax.shard_map(
        functools.partial(body, nc, nz), mesh=mesh, in_specs=in_specs, out_specs=out_specs, check_vma=False
    )
```

time: 80.7 us -> 60.9 us (0.75)
  the two profiles are of different devices: /device:TPU:32 before, /device:TPU:1 now
where the time goes in v2:
time: 60.9 us; the launch traced here: 60.8 us
  Pallas kernels  60.2 us (99%)
  between operations  0.64 us (1%)
    pallas_call x1, Pallas kernels, body(): pl.pallas_call(functools.partial(kernel, nc, nz, names), out_shape=outs,...  58.3 us
    pallas_call x1, Pallas kernels, body(): pl.pallas_call(place, out_shape=outs, in_specs=[pl.BlockSpec(memory_space...  1.84 us

profile of v2, /device:TPU:1, one launch (start us, length us, event | category | flops | bytes accessed | tf_op | source)
XLA Modules:
  0.0 60.8 jit_solution(10101593447831321732)
XLA Ops:
  0.6 58.3 %shard_map.165 = (f32[4,8192]{1,0:T(4,128)}, f32[4,6400]{1,0:T(4,128)}, f32[4,8192]{1,0:T(4,128)}, f32[4,6400]{1,0:T(4,128)}) custom-call(f32[4,8192]{1,0:T(4,128)} %refs_0_.1, f32[4,6400]{1,0:T(4,128)} %refs_1_.1, f32[1,8192]{1,0:T(1,128)} %bitcast.5, s32[1,8192]{1,0:T(1,128)} %bitcast.6, s32[1,8192]{1,0:T(1,128)} %bitcast.7, s32[1,32]{1,0:T(1,128)} %bitcast.9, ...), custom_call_target="tpu_custom_call" | custom-call | flops 4000000000 | bytes 10000000 | tf_op jit(solution)/shard_map/pallas_call | solution.py:645
  59.0 1.8 %shard_map.166 = (f32[4,8192]{1,0:T(4,128)}, f32[4,6400]{1,0:T(4,128)}, f32[4,8192]{1,0:T(4,128)}, f32[4,6400]{1,0:T(4,128)}) custom-call(f32[4,8192]{1,0:T(4,128)} %get-tuple-element.8.refs_0_, f32[4,6400]{1,0:T(4,128)} %get-tuple-element.9.refs_1_, f32[4,8192]{1,0:T(4,128)} %get-tuple-element.10.refs_2_, f32[4,6400]{1,0:T(4,128)} %get-tuple-element.11.refs_3_), custom_call_target="tpu_custom_call" | custom-call | tf_op jit(solution)/shard_map/pallas_call | solution.py:654

commit v3 on v2

--- a/solution.py
+++ b/solution.py
@@ -138,13 +138,14 @@
         ny = min(4, nc // 2)
         nx = nc // (2 * ny)
         x, y, core = c // (2 * ny), c // 2 % ny, c % 2
-
-        @pl.loop(0, nc)
-        def _(t):
-            to_x = lax.rem(x + t // (2 * ny) + nx // 2, nx)
-            to_y = lax.rem(y + t // 2 % ny + ny // 2, ny)
-            other = (to_x * ny + to_y) * 2 + lax.rem(core + t, 2)
-            pl.when(other != c)(lambda: act(other))
+        xs = [lax.rem(x + (i + nx // 2) % nx, nx) * (2 * ny) for i in range(nx)]
+        ys = [lax.rem(y + (i + ny // 2) % ny, ny) * 2 for i in range(ny)]
+        cores = [core, 1 - core]
+        for i in range(nx):
+            for j in range(ny):
+                for k in range(2):
+                    if (i + nx // 2) % nx or (j + ny // 2) % ny or k:
+                        act(xs[i] + ys[j] + cores[k])
 
     def to_cohort(src, dst, send_sem, recv_sem):
         around(lambda other: send(src, dst, send_sem, recv_sem, (other, z)))
@@ -159,7 +160,7 @@
         at = lax.rem(j + lows // 2 - z * (prow // 8) + reach * (prow // 8), lows // 2)
         return pl.ds(pl.multiple_of(at * 8, 8), 8)
 
-    @pl.loop(0, lows // 2)
+    @pl.loop(0, lows // 2, unroll=4)
     def _(j):
         here = pl.ds(pl.multiple_of(j * 2 * HI, 2 * HI), 2 * HI)
         slot = (lax.broadcasted_iota(jnp.int32, (1, 2 * HI), 1) + j * 2 * HI).astype(F32)
@@ -269,8 +270,11 @@
                     r.up_ssem.at[step], r.up_rsem.at[step], (cohort_at(offset), z),
                 )
 
-        for i in range(SPAN):
-            pl.when(l == i)(functools.partial(to, readers[i]))
+        if isinstance(l, int):
+            to(readers[l])
+        else:
+            for i in range(SPAN):
+                pl.when(l == i)(functools.partial(to, readers[i]))
 
     def send_own(step, src):
         for l in reversed(range(SPAN)):
@@ -285,6 +289,7 @@
     row4 = lax.broadcasted_iota(jnp.int32, (4, 128), 0)
     at_owner = jnp.where(is_owner, 1.0, 0.0)
     every = (near_part, far_part) if far_rows else (near_part,)
+    whole = (0, rows)
 
     send_own(0, r.z_a0.at[:, my_slots])
     for load in loads[3:]:
@@ -295,8 +300,7 @@
     for step in range(2):
         if step == 0:
             marker_product(0)
-            for which in every:
-                load_field(0, which)
+            load_field(0, whole)
 
             @pl.loop(0, SPAN)
             def _(i):
@@ -306,7 +310,7 @@
                     hot, key = one_hot(r.idx_recv[l, k])
                     r.hot[2 * l + k] = hot
                     r.key[2 * l + k] = key
-                r.up_own[0, l] = halves(sum(gather_all(which, l) for which in every))
+                r.up_own[0, l] = halves(gather_all(whole, l))
                 send_sums_up(0, l)
                 r.factor[l] = factor_of(r.idx_recv[l, 0], r.idx_recv[l, 1])
 
@@ -318,17 +322,14 @@
                 wait(r.field.at[1, pl.ds(0, near_rows - prow), :], r.fl_rsem.at[0])
             load_field(1, near_part)
 
-            @pl.loop(0, SPAN)
-            def _(l):
+            for l in range(SPAN):
                 r.partial[l] = gather_all(near_part, l)
 
             if far_rows:
                 wait(r.field.at[1, near_rows:, :], r.fl_rsem.at[1])
                 load_field(1, far_part)
 
-            @pl.loop(0, SPAN)
-            def _(i):
-                l = SPAN - 1 - i
+            for l in reversed(range(SPAN)):
                 total = r.partial[l]
                 if far_rows:
                     total = total + gather_all(far_part, l)
@@ -350,30 +351,47 @@
             )
             r.q_a[:, my_slots] = r.image_a[...]
 
-        dir_g = halves(sum(gather(which, r.hot_g[...], r.key_g[...]) for which in every))
+            @pl.when(is_owner)
+            def _():
+                r.q_s[:, own_at] = r.image_s[...]
+                mine = r.q_s.at[:, own_at]
+                to_cohort(mine, mine, r.qs_ssem, r.qs_rsem)
+
+        dir_g = halves(sum(gather(which, r.hot_g[...], r.key_g[...]) for which in (every if step else (whole,))))
+
+        def tie_up():
+            wait(r.mk.at[step, pl.ds(0, nz - 1)], r.mk_rsem.at[step])
+            mismatch = dir_g - jnp.sum(r.mk[step], axis=0)
+            tied = mix(coup, mismatch)
+
+            both = stacked_split(tied)
+
+            @pl.loop(0, chunks)
+            def _(j):
+                at = pl.ds(pl.multiple_of(j * chunk, chunk), chunk)
+                sums = jnp.dot(both, r.geno_hi[j], preferred_element_type=F32) + jnp.dot(
+                    both, r.geno_lo[j], preferred_element_type=F32
+                )
+                r.part_s[step, :, at] = sums[0:TRAITS, :] + sums[TRAITS : 2 * TRAITS, :]
+
+            r.sum_s[step, c] = r.part_s[step, :, own_at]
+
+            def send_sums(other):
+                @pl.when(other < owners)
+                def _():
+                    send(
+                        r.part_s.at[step, :, pl.ds(pl.multiple_of(other * OWN, OWN), OWN)],
+                        r.sum_s.at[step, c], r.ss_ssem.at[step], r.ss_rsem.at[step], (other, z),
+                    )
+
+            around(send_sums)
+            return mismatch, tied
+
+        if step == 0:
+            mismatch, tied = tie_up()
 
         wait(r.own_recv.at[step], r.own_rsem.at[step])
         wait(r.up_recv.at[step], r.up_rsem.at[step])
-        others = ((1, 4), (2, 6), (7, 8))
-        for l in range(SPAN):
-            parents = r.up_own[step, l] + r.up_recv[step, others[l][0]] + r.up_recv[step, others[l][1]]
-            terms = r.factor[l] * (r.own_recv[step, l] - 0.5 * parents)
-            r.terms[l] = -0.5 * mix(gen_inv, terms)
-        r.acc_b[...] = jnp.zeros_like(r.acc_b)
-
-        @pl.loop(0, SPAN)
-        def _(l):
-            r.acc_b[...] += scatter((0, rows), r.terms[l], r.hot[2 * l], r.key[2 * l]) + scatter(
-                (0, rows), r.terms[l], r.hot[2 * l + 1], r.key[2 * l + 1]
-            )
-
-        r.back[step] = r.acc_b[0:rows, :] + r.acc_b[rows : 2 * rows, :]
-        to_snp(
-            lambda k: r.back.at[step, pl.ds((k + reach) % nz * prow, prow), :],
-            lambda k: r.back_recv.at[step, k], r.bk_ssem.at[step], lambda k: r.bk_rsem.at[step], order,
-        )
-        r.back_recv[step, 0] = r.back[step, my_rows, :]
-
         own = r.z_a0[:, my_slots] if step == 0 else r.y_own[...]
         deviation = own - 0.5 * (r.up_recv[step, 0] + r.up_recv[step, 3] + r.up_recv[step, 5])
         mixed = mix(gen_inv, factor * deviation)
@@ -409,42 +427,42 @@
         my_dots = r.dot_z.at[step, z]
         to_snp(lambda k: my_dots, lambda k: my_dots, r.dz_ssem.at[step], lambda k: r.dz_rsem.at[step], order)
 
-        wait(r.mk.at[step, pl.ds(0, nz - 1)], r.mk_rsem.at[step])
-        mismatch = dir_g - jnp.sum(r.mk[step], axis=0)
-        tied = mix(coup, mismatch)
-
-        both = stacked_split(tied)
-
-        @pl.loop(0, chunks)
-        def _(j):
-            at = pl.ds(pl.multiple_of(j * chunk, chunk), chunk)
-            sums = jnp.dot(both, r.geno_hi[j], preferred_element_type=F32) + jnp.dot(
-                both, r.geno_lo[j], preferred_element_type=F32
+        others = ((1, 4), (2, 6), (7, 8))
+        for l in range(SPAN):
+            parents = r.up_own[step, l] + r.up_recv[step, others[l][0]] + r.up_recv[step, others[l][1]]
+            terms = r.factor[l] * (r.own_recv[step, l] - 0.5 * parents)
+            r.terms[l] = -0.5 * mix(gen_inv, terms)
+        r.acc_b[...] = jnp.zeros_like(r.acc_b)
+
+        @pl.loop(0, SPAN)
+        def _(l):
+            r.acc_b[...] += scatter(whole, r.terms[l], r.hot[2 * l], r.key[2 * l]) + scatter(
+                whole, r.terms[l], r.hot[2 * l + 1], r.key[2 * l + 1]
             )
-            r.part_s[step, :, at] = sums[0:TRAITS, :] + sums[TRAITS : 2 * TRAITS, :]
-
-        r.sum_s[step, c] = r.part_s[step, :, own_at]
-
-        def send_sums(other):
-            @pl.when(other < owners)
-            def _():
-                send(
-                    r.part_s.at[step, :, pl.ds(pl.multiple_of(other * OWN, OWN), OWN)],
-                    r.sum_s.at[step, c], r.ss_ssem.at[step], r.ss_rsem.at[step], (other, z),
-                )
-
-        around(send_sums)
-
-        if step == 0:
-            r.mismatch[...] = mismatch
-            tied_row = fold(mismatch * tied)
-        else:
-            mismatch = r.mismatch[...] - alpha0 * mismatch
-            tied_row = fold(mismatch * mix(coup, mismatch))
-        wait(r.dot_z.at[step, pl.ds(0, nz - 1)], r.dz_rsem.at[step])
-        r.dot_c[step, c] = jnp.sum(r.dot_z[step], axis=0) + jnp.where(row4 == 1, tied_row, 0.0)
-        my_dots = r.dot_c.at[step, c]
-        to_cohort(my_dots, my_dots, r.dc_ssem.at[step], r.dc_rsem.at[step])
+
+        r.back[step] = r.acc_b[0:rows, :] + r.acc_b[rows : 2 * rows, :]
+        to_snp(
+            lambda k: r.back.at[step, pl.ds((k + reach) % nz * prow, prow), :],
+            lambda k: r.back_recv.at[step, k], r.bk_ssem.at[step], lambda k: r.bk_rsem.at[step], order,
+        )
+        r.back_recv[step, 0] = r.back[step, my_rows, :]
+
+        if step == 1:
+            mismatch, tied = tie_up()
+        def send_dots():
+            if step == 0:
+                r.mismatch[...] = mismatch
+                tied_row = fold(mismatch * tied)
+            else:
+                apart = r.mismatch[...] - alpha0 * mismatch
+                tied_row = fold(apart * mix(coup, apart))
+            wait(r.dot_z.at[step, pl.ds(0, nz - 1)], r.dz_rsem.at[step])
+            r.dot_c[step, c] = jnp.sum(r.dot_z[step], axis=0) + jnp.where(row4 == 1, tied_row, 0.0)
+            my_dots = r.dot_c.at[step, c]
+            to_cohort(my_dots, my_dots, r.dc_ssem.at[step], r.dc_rsem.at[step])
+
+        if step == 1:
+            send_dots()
 
         tie = scatter((reach * prow, prow), tied, r.hot_g[...], r.key_g[...])
         local_a = local_a + slots_of(tie[0:prow, :] + tie[prow : 2 * prow, :])
@@ -466,6 +484,7 @@
             r.y_own[...] = y_a
             r.image_a[...] = image_a
             send_own(1, r.y_own)
+            send_dots()
         else:
             r.w_own[...] = image_a
             landing = r.w_a.at[:, my_slots]
@@ -493,9 +512,6 @@
                 r.w_s[:, own_at] = image_s
                 mine = r.w_s.at[:, own_at]
                 to_cohort(mine, mine, r.rs_ssem, r.rs_rsem)
-                r.q_s[:, own_at] = r.image_s[...]
-                mine = r.q_s.at[:, own_at]
-                to_cohort(mine, mine, r.qs_ssem, r.qs_rsem)
 
     wait(r.dot_c.at[1, pl.ds(0, nc - 1)], r.dc_rsem.at[1])
     dots = jnp.sum(r.dot_c[1], axis=0)
@@ -508,7 +524,7 @@
     wait(r.q_a.at[:, pl.ds(0, slots - part)], r.qa_rsem)
     wait(r.w_a.at[:, pl.ds(0, slots - part)], r.ra_rsem)
 
-    @pl.loop(0, lows // 2)
+    @pl.loop(0, lows // 2, unroll=4)
     def _(j):
         here = pl.ds(pl.multiple_of(j * 2 * HI, 2 * HI), 2 * HI)
         y = r.field[1, place_of(j), :]
@@ -526,7 +542,7 @@
         def _():
             wait(full, sem)
 
-    @pl.loop(0, owners)
+    @pl.loop(0, owners, unroll=5)
     def _(j):
         here = pl.ds(pl.multiple_of(j * OWN, OWN), OWN)
         r.out_sol_s[:, here] = once * r.z_s[0, :, here] - twice * r.z_s[1, :, here]
@@ -570,8 +586,7 @@
     slots, snps, genos = rhs_a.shape[1], rhs_s.shape[1], geno_idx.shape[0]
     part = slots // nz
     rows = slots // HI * TRAITS
-    chunk = next(k for k in (1280, 1024, 512, 256) if snps % k == 0)
-    chunks = snps // chunk
+    chunk, chunks = snps, 1
     vmem, dma = pltpu.VMEM, pltpu.SemaphoreType.DMA
     inputs = dict(
         rhs_a=rhs_a, rhs_s=rhs_s, weight=weight[None], sire=sire[None], dam=dam[None], sizes=sizes[None],

time: 60.9 us -> 55.8 us (0.916)
  Pallas kernels: 60.2 us -> 55 us
    pallas_call x1, Pallas kernels: 58.3 us -> 53.2 us  [body(): pl.pallas_call(functools.partial(kernel, nc, nz, names), out_shape=outs,...]
where the time goes in v3:
time: 55.8 us; the launch traced here: 55.7 us
  Pallas kernels  55 us (99%)
  between operations  0.64 us (1%)
    pallas_call x1, Pallas kernels, body(): pl.pallas_call(functools.partial(kernel, nc, nz, names), out_shape=outs,...  53.2 us
    pallas_call x1, Pallas kernels, body(): pl.pallas_call(place, out_shape=outs, in_specs=[pl.BlockSpec(memory_space...  1.84 us

profile of v3, /device:TPU:1, one launch (start us, length us, event | category | flops | bytes accessed | tf_op | source)
XLA Modules:
  0.0 55.7 jit_solution(11900016266816352688)
XLA Ops:
  0.6 53.2 %shard_map.165 = (f32[4,8192]{1,0:T(4,128)}, f32[4,6400]{1,0:T(4,128)}, f32[4,8192]{1,0:T(4,128)}, f32[4,6400]{1,0:T(4,128)}) custom-call(f32[4,8192]{1,0:T(4,128)} %refs_0_.1, f32[4,6400]{1,0:T(4,128)} %refs_1_.1, f32[1,8192]{1,0:T(1,128)} %bitcast.5, s32[1,8192]{1,0:T(1,128)} %bitcast.6, s32[1,8192]{1,0:T(1,128)} %bitcast.7, s32[1,32]{1,0:T(1,128)} %bitcast.9, ...), custom_call_target="tpu_custom_call" | custom-call | flops 4000000000 | bytes 10000000 | tf_op jit(solution)/shard_map/pallas_call | solution.py:660
  53.8 1.8 %shard_map.166 = (f32[4,8192]{1,0:T(4,128)}, f32[4,6400]{1,0:T(4,128)}, f32[4,8192]{1,0:T(4,128)}, f32[4,6400]{1,0:T(4,128)}) custom-call(f32[4,8192]{1,0:T(4,128)} %get-tuple-element.8.refs_0_, f32[4,6400]{1,0:T(4,128)} %get-tuple-element.9.refs_1_, f32[4,8192]{1,0:T(4,128)} %get-tuple-element.10.refs_2_, f32[4,6400]{1,0:T(4,128)} %get-tuple-element.11.refs_3_), custom_call_target="tpu_custom_call" | custom-call | tf_op jit(solution)/shard_map/pallas_call | solution.py:669

commit v4 on v3

--- a/solution.py
+++ b/solution.py
@@ -47,8 +47,7 @@
 
 def z_plan(nz):
     order = sorted(range(1, nz), key=lambda k: -min(k, nz - k))
-    reach = nz // 4
-    return order, reach, 2 * reach + 1 if nz >= 4 else nz
+    return order, nz // 4
 
 
 def kernel(nc, nz, names, *refs):
@@ -68,9 +67,7 @@
     is_owner = c < owners
     own_at = pl.ds(pl.multiple_of(own_block * OWN, OWN), OWN)
     my_slots = pl.ds(pl.multiple_of(z * part, part), part)
-    order, reach, nears = z_plan(nz)
-    near_rows = nears * prow
-    far_rows = rows - near_rows
+    order, reach = z_plan(nz)
     my_rows = slice(reach * prow, (reach + 1) * prow)
 
     def cohort_at(k):
@@ -93,8 +90,6 @@
         (r.in_geno_idx, r.geno_idx),
         (r.in_rhs_s, r.rhs_s),
         (r.in_pre_s, r.pre_s),
-        (r.in_sire.at[:, my_slots], r.idx_own.at[0]),
-        (r.in_dam.at[:, my_slots], r.idx_own.at[1]),
         (r.in_weight.at[:, my_slots], r.weight),
         (r.in_gen_inv, r.gen_inv),
         (r.in_res_inv, r.res_inv),
@@ -222,8 +217,6 @@
         place = jnp.where(here, around_low, -8)
         return hot, place - jnp.right_shift(lax.broadcasted_iota(jnp.int32, (8, n), 0), 2)
 
-    near_part, far_part = (0, near_rows), (near_rows, far_rows)
-
     def load_field(step, which):
         first, count = which
         high, low = split(r.field[step, first : first + count, :])
@@ -260,7 +253,7 @@
     def slots_of(block):
         return jnp.concatenate([block[i : i + TRAITS, :] for i in range(0, prow, TRAITS)], axis=1)
 
-    readers = (((1, 0), (-1, 6), (-2, 8)), ((1, 1), (2, 3), (-1, 7)), ((1, 2), (2, 4), (3, 5)))
+    readers = (((-2, 4), (-1, 3)), ((1, 0), (-1, 5)), ((2, 2), (1, 1)))
 
     def send_sums_up(step, l):
         def to(readers_l):
@@ -288,23 +281,19 @@
 
     row4 = lax.broadcasted_iota(jnp.int32, (4, 128), 0)
     at_owner = jnp.where(is_owner, 1.0, 0.0)
-    every = (near_part, far_part) if far_rows else (near_part,)
     whole = (0, rows)
 
     send_own(0, r.z_a0.at[:, my_slots])
     for load in loads[3:]:
         load.wait()
     gen_inv, res_inv, coup, prior = (x[...] for x in (r.gen_inv, r.res_inv, r.coup, r.prior))
-    factor = factor_of(r.idx_own[0], r.idx_own[1])
 
     for step in range(2):
         if step == 0:
             marker_product(0)
             load_field(0, whole)
 
-            @pl.loop(0, SPAN)
-            def _(i):
-                l = SPAN - 1 - i
+            for l in reversed(range(SPAN)):
                 wait(r.idx_recv.at[l], r.idx_rsem.at[l])
                 for k in range(2):
                     hot, key = one_hot(r.idx_recv[l, k])
@@ -318,21 +307,11 @@
             r.hot_g[...] = hot
             r.key_g[...] = key
         else:
-            if nears > 1:
-                wait(r.field.at[1, pl.ds(0, near_rows - prow), :], r.fl_rsem.at[0])
-            load_field(1, near_part)
-
-            for l in range(SPAN):
-                r.partial[l] = gather_all(near_part, l)
-
-            if far_rows:
-                wait(r.field.at[1, near_rows:, :], r.fl_rsem.at[1])
-                load_field(1, far_part)
+            wait(r.field.at[1, pl.ds(0, rows - prow), :], r.fl_rsem)
+            load_field(1, whole)
 
             for l in reversed(range(SPAN)):
-                total = r.partial[l]
-                if far_rows:
-                    total = total + gather_all(far_part, l)
+                total = gather_all(whole, l)
                 r.up_own[1, l] = halves(total)
                 send_sums_up(1, l)
 
@@ -357,7 +336,7 @@
                 mine = r.q_s.at[:, own_at]
                 to_cohort(mine, mine, r.qs_ssem, r.qs_rsem)
 
-        dir_g = halves(sum(gather(which, r.hot_g[...], r.key_g[...]) for which in (every if step else (whole,))))
+        dir_g = halves(gather(whole, r.hot_g[...], r.key_g[...]))
 
         def tie_up():
             wait(r.mk.at[step, pl.ds(0, nz - 1)], r.mk_rsem.at[step])
@@ -384,24 +363,35 @@
                         r.sum_s.at[step, c], r.ss_ssem.at[step], r.ss_rsem.at[step], (other, z),
                     )
 
-            around(send_sums)
-            return mismatch, tied
+            return mismatch, tied, send_sums
 
         if step == 0:
-            mismatch, tied = tie_up()
+            mismatch, tied, send_sums = tie_up()
 
         wait(r.own_recv.at[step], r.own_rsem.at[step])
         wait(r.up_recv.at[step], r.up_rsem.at[step])
+        others = ((0, 2), (1, 3), (5, 4))
+        for l in range(SPAN):
+            parents = r.up_own[step, l] + r.up_recv[step, others[l][0]] + r.up_recv[step, others[l][1]]
+            apart_l = r.own_recv[step, l] - 0.5 * parents
+            mixed_l = mix(gen_inv, r.factor[l] * apart_l)
+            r.terms[l] = -0.5 * mixed_l
+            if l == 0:
+                deviation, mixed = apart_l, mixed_l
+                r.mixed[step] = mixed
+                send(
+                    r.mixed.at[step], r.down_recv.at[step],
+                    r.down_ssem.at[step], r.down_rsem.at[step], (cohort_at(1), z),
+                )
+
         own = r.z_a0[:, my_slots] if step == 0 else r.y_own[...]
-        deviation = own - 0.5 * (r.up_recv[step, 0] + r.up_recv[step, 3] + r.up_recv[step, 5])
-        mixed = mix(gen_inv, factor * deviation)
-        local_a = r.weight[...] * mix(res_inv, own) + mixed
+        local_a = r.weight[...] * mix(res_inv, own)
         own_s = r.z_s[step, :, own_at]
         local_s = mix(prior, own_s)
         if step == 0:
             r.local_s[...] = local_s
             r.deviation[...] = deviation
-            curve = fold(own * (local_a - mixed) + deviation * mixed) + at_owner * fold(own_s * local_s)
+            curve = fold(own * local_a + deviation * mixed) + at_owner * fold(own_s * local_s)
             gamma_row = fold(own * r.res_a0[:, my_slots]) + at_owner * fold(own_s * r.rhs_s[:, own_at])
             cross_row = jnp.zeros((1, 128), F32)
         else:
@@ -416,7 +406,7 @@
             gamma_row = fold(z_own * res_a1) + at_owner * fold(zs_own * res_s1)
             cross_row = fold(z_own * r.image_a[...]) + at_owner * fold(zs_own * r.image_s[...])
             deviation = r.deviation[...] - alpha0 * deviation
-            z_mixed = mix(gen_inv, factor * deviation)
+            z_mixed = mix(gen_inv, r.factor[0] * deviation)
             record = r.weight[...] * mix(res_inv, z_own)
             curve = fold(z_own * record + deviation * z_mixed) + at_owner * fold(
                 zs_own * (r.local_s[...] - alpha0 * local_s)
@@ -427,11 +417,6 @@
         my_dots = r.dot_z.at[step, z]
         to_snp(lambda k: my_dots, lambda k: my_dots, r.dz_ssem.at[step], lambda k: r.dz_rsem.at[step], order)
 
-        others = ((1, 4), (2, 6), (7, 8))
-        for l in range(SPAN):
-            parents = r.up_own[step, l] + r.up_recv[step, others[l][0]] + r.up_recv[step, others[l][1]]
-            terms = r.factor[l] * (r.own_recv[step, l] - 0.5 * parents)
-            r.terms[l] = -0.5 * mix(gen_inv, terms)
         r.acc_b[...] = jnp.zeros_like(r.acc_b)
 
         @pl.loop(0, SPAN)
@@ -448,7 +433,8 @@
         r.back_recv[step, 0] = r.back[step, my_rows, :]
 
         if step == 1:
-            mismatch, tied = tie_up()
+            mismatch, tied, send_sums = tie_up()
+        around(send_sums)
         def send_dots():
             if step == 0:
                 r.mismatch[...] = mismatch
@@ -466,6 +452,8 @@
 
         tie = scatter((reach * prow, prow), tied, r.hot_g[...], r.key_g[...])
         local_a = local_a + slots_of(tie[0:prow, :] + tie[prow : 2 * prow, :])
+        wait(r.down_recv.at[step], r.down_rsem.at[step])
+        local_a = local_a + r.down_recv[step]
         wait(r.back_recv.at[step, pl.ds(0, nz - 1)], r.bk_rsem.at[step])
         image_a = local_a + slots_of(jnp.sum(r.back_recv[step], axis=0))
         if step == 0:
@@ -479,7 +467,7 @@
             mine = r.field.at[1, my_rows, :]
             to_snp(
                 lambda k: mine, lambda k: r.field.at[1, pl.ds((reach - k) % nz * prow, prow), :],
-                r.fl_ssem, lambda k: r.fl_rsem.at[0 if (reach - k) % nz < nears else 1], order,
+                r.fl_ssem, lambda k: r.fl_rsem, order,
             )
             r.y_own[...] = y_a
             r.image_a[...] = image_a
@@ -487,9 +475,9 @@
             send_dots()
         else:
             r.w_own[...] = image_a
-            landing = r.w_a.at[:, my_slots]
+            landing = r.out_w_a.at[:, my_slots]
             to_snp(lambda k: r.w_own, lambda k: landing, r.ra_ssem, lambda k: r.ra_rsem, order)
-            r.w_a[:, my_slots] = image_a
+            pltpu.make_async_copy(r.w_own, landing, r.out_sem.at[5]).start()
 
         @pl.when(is_owner)
         def _():
@@ -509,9 +497,10 @@
 
             @pl.when(is_owner)
             def _():
-                r.w_s[:, own_at] = image_s
-                mine = r.w_s.at[:, own_at]
-                to_cohort(mine, mine, r.rs_ssem, r.rs_rsem)
+                r.ws_own[...] = image_s
+                landing = r.out_w_s.at[:, own_at]
+                to_cohort(r.ws_own, landing, r.rs_ssem, r.rs_rsem)
+                pltpu.make_async_copy(r.ws_own, landing, r.out_sem.at[6]).start()
 
     wait(r.dot_c.at[1, pl.ds(0, nc - 1)], r.dc_rsem.at[1])
     dots = jnp.sum(r.dot_c[1], axis=0)
@@ -522,18 +511,16 @@
     once = alpha0 + alpha1 * (1.0 + beta)
     twice = alpha1 * alpha0
     wait(r.q_a.at[:, pl.ds(0, slots - part)], r.qa_rsem)
-    wait(r.w_a.at[:, pl.ds(0, slots - part)], r.ra_rsem)
 
     @pl.loop(0, lows // 2, unroll=4)
     def _(j):
         here = pl.ds(pl.multiple_of(j * 2 * HI, 2 * HI), 2 * HI)
         y = r.field[1, place_of(j), :]
         y = jnp.concatenate([y[0:TRAITS, :], y[TRAITS:8, :]], axis=1)
-        r.out_sol_a[:, here] = once * r.z_a0[:, here] - twice * y
-        r.out_ra[:, here] = r.res_a0[:, here] - once * r.q_a[:, here] + twice * r.w_a[:, here]
-
-    for full, sem in ((r.q_s, r.qs_rsem), (r.w_s, r.rs_rsem)):
-
+        r.sol_a[:, here] = once * r.z_a0[:, here] - twice * y
+        r.left_a[:, here] = r.res_a0[:, here] - once * r.q_a[:, here]
+
+    def arrived(full, sem):
         @pl.when(is_owner)
         def _():
             wait(full.at[:, pl.ds(0, (owners - 1) * OWN)], sem)
@@ -542,17 +529,33 @@
         def _():
             wait(full, sem)
 
+    arrived(r.q_s, r.qs_rsem)
+
     @pl.loop(0, owners, unroll=5)
     def _(j):
         here = pl.ds(pl.multiple_of(j * OWN, OWN), OWN)
-        r.out_sol_s[:, here] = once * r.z_s[0, :, here] - twice * r.z_s[1, :, here]
-        r.out_rs[:, here] = r.rhs_s[:, here] - once * r.q_s[:, here] + twice * r.w_s[:, here]
+        r.sol_s[:, here] = once * r.z_s[0, :, here] - twice * r.z_s[1, :, here]
+        r.left_s[:, here] = r.rhs_s[:, here] - once * r.q_s[:, here]
+
+    r.scale[...] = jnp.broadcast_to(twice, r.scale.shape)
+    stores = [
+        pltpu.make_async_copy(src, dst, r.out_sem.at[i])
+        for i, (src, dst) in enumerate(
+            (
+                (r.sol_a, r.out_sol_a), (r.sol_s, r.out_sol_s), (r.left_a, r.out_left_a),
+                (r.left_s, r.out_left_s), (r.scale, r.out_scale),
+            )
+        )
+    ]
+    for store in stores:
+        store.start()
 
     for l in range(SPAN):
-        wait(r.idx_own, r.idx_ssem.at[l])
+        wait(r.idx_recv.at[l], r.idx_ssem.at[l])
     for step in range(2):
         wait(r.up_recv.at[step], r.up_ssem.at[step])
         wait(r.own_recv.at[step], r.own_ssem.at[step])
+        wait(r.mixed.at[step], r.down_ssem.at[step])
         wait(r.mk.at[step, pl.ds(0, nz - 1)], r.mk_ssem.at[step])
         wait(r.dot_z.at[step, pl.ds(0, nz - 1)], r.dz_ssem.at[step])
         wait(r.dot_c.at[step, pl.ds(0, nc - 1)], r.dc_ssem.at[step])
@@ -573,13 +576,25 @@
 
     wait(r.field.at[1, pl.ds(0, rows - prow), :], r.fl_ssem)
     wait(r.q_a.at[:, pl.ds(0, slots - part)], r.qa_ssem)
-    wait(r.w_a.at[:, pl.ds(0, slots - part)], r.ra_ssem)
-
-
-def place(*refs):
-    half = len(refs) // 2
-    for i in range(half):
-        refs[half + i][...] = refs[i][...]
+    wait(r.q_a.at[:, pl.ds(0, slots - part)], r.ra_ssem)
+    for store in stores:
+        store.wait()
+    pltpu.make_async_copy(r.w_own, r.out_w_a.at[:, my_slots], r.out_sem.at[5]).wait()
+    wait(r.sol_a.at[:, pl.ds(0, slots - part)], r.ra_rsem)
+
+    @pl.when(is_owner)
+    def _():
+        pltpu.make_async_copy(r.ws_own, r.out_w_s.at[:, own_at], r.out_sem.at[6]).wait()
+
+    arrived(r.sol_s, r.rs_rsem)
+
+
+def place(sol_a, sol_s, left_a, left_s, w_a, w_s, scale, out_sol_a, out_sol_s, out_ra, out_rs):
+    twice = scale[0:1, 0:1]
+    out_sol_a[...] = sol_a[...]
+    out_sol_s[...] = sol_s[...]
+    out_ra[...] = left_a[...] + twice * w_a[...]
+    out_rs[...] = left_s[...] + twice * w_s[...]
 
 
 def body(nc, nz, rhs_a, rhs_s, weight, sire, dam, sizes, geno_idx, genotypes, pre_a, pre_s, *small):
@@ -608,7 +623,6 @@
         geno_f32=vmem((chunks, genos, chunk), F32),
         geno_hi=vmem((chunks, genos, chunk), BF16),
         geno_lo=vmem((chunks, genos, chunk), BF16),
-        idx_own=vmem((2, 1, part), jnp.int32),
         idx_recv=vmem((SPAN, 2, 1, part), jnp.int32),
         hot=vmem((2 * SPAN, HI, part), BF16),
         key=vmem((2 * SPAN, 8, part), jnp.int32),
@@ -618,7 +632,6 @@
         z_a0=vmem((TRAITS, slots), F32),
         field=vmem((2, rows, HI), F32),
         field_bf=vmem((2 * rows, HI), BF16),
-        partial=vmem((SPAN, 8, part), F32),
         z_s=vmem((2, TRAITS, snps), F32),
         acc_m=vmem((2 * TRAITS, genos), F32),
         mk=vmem((2, nz, TRAITS, genos), F32),
@@ -626,7 +639,9 @@
         sum_s=vmem((2, nc, TRAITS, OWN), F32),
         factor=vmem((SPAN, 1, part), F32),
         up_own=vmem((2, SPAN, TRAITS, part), F32),
-        up_recv=vmem((2, 9, TRAITS, part), F32),
+        up_recv=vmem((2, 6, TRAITS, part), F32),
+        mixed=vmem((2, TRAITS, part), F32),
+        down_recv=vmem((2, TRAITS, part), F32),
         own_recv=vmem((2, SPAN, TRAITS, part), F32),
         terms=vmem((SPAN, TRAITS, part), F32),
         dot_z=vmem((2, nz, 4, 128), F32),
@@ -642,26 +657,30 @@
         local_s=vmem((TRAITS, OWN), F32),
         image_s=vmem((TRAITS, OWN), F32),
         q_a=vmem((TRAITS, slots), F32),
-        w_a=vmem((TRAITS, slots), F32),
+        sol_a=vmem((TRAITS, slots), F32),
+        left_a=vmem((TRAITS, slots), F32),
         q_s=vmem((TRAITS, snps), F32),
-        w_s=vmem((TRAITS, snps), F32),
-        load_sem=dma((13 + chunks,)),
+        ws_own=vmem((TRAITS, OWN), F32),
+        sol_s=vmem((TRAITS, snps), F32),
+        left_s=vmem((TRAITS, snps), F32),
+        scale=vmem((8, 128), F32),
+        out_sem=dma((7,)),
+        load_sem=dma((11 + chunks,)),
     )
     for name, shape in dict(
-        idx=(SPAN,), up=(2,), own=(2,), mk=(2,), ss=(2,), dz=(2,), dc=(2,), bk=(2,), zs=(), rs=(), qs=(), qa=(), ra=(),
+        idx=(SPAN,), up=(2,), own=(2,), down=(2,), mk=(2,), ss=(2,), dz=(2,), dc=(2,), bk=(2,), zs=(), rs=(), qs=(), qa=(), fl=(), ra=(),
     ).items():
         scratch[name + "_ssem"] = dma(shape)
         scratch[name + "_rsem"] = dma(shape)
-    scratch |= dict(fl_ssem=dma(()), fl_rsem=dma((2,)))
     names = ["in_" + name for name in inputs]
-    names += ["out_sol_a", "out_sol_s", "out_ra", "out_rs"] + list(scratch)
+    names += ["out_sol_a", "out_sol_s", "out_left_a", "out_left_s", "out_w_a", "out_w_s", "out_scale"] + list(scratch)
     outs = [jax.ShapeDtypeStruct(x.shape, F32) for x in (rhs_a, rhs_s, rhs_a, rhs_s)]
     limit = 56 * 1024 * 1024
     results = pl.pallas_call(
         functools.partial(kernel, nc, nz, names),
-        out_shape=outs,
+        out_shape=outs + outs[:2] + [jax.ShapeDtypeStruct((8, 128), F32)],
         in_specs=[pl.BlockSpec(memory_space=pl.ANY)] * len(inputs),
-        out_specs=[pl.BlockSpec(memory_space=pltpu.VMEM)] * 4,
+        out_specs=[pl.BlockSpec(memory_space=pl.ANY)] * 7,
         scratch_shapes=list(scratch.values()),
         compiler_params=pltpu.CompilerParams(collective_id=0, has_side_effects=True, vmem_limit_bytes=limit),
         cost_estimate=pl.CostEstimate(flops=4 * 10**9, bytes_accessed=10**7, transcendentals=0),
@@ -669,7 +688,7 @@
     return pl.pallas_call(
         place,
         out_shape=outs,
-        in_specs=[pl.BlockSpec(memory_space=pltpu.VMEM)] * 4,
+        in_specs=[pl.BlockSpec(memory_space=pltpu.VMEM)] * 7,
         out_specs=[pl.BlockSpec(memory_space=pltpu.VMEM)] * 4,
     )(*results)
 

time: 55.8 us -> 53.9 us (0.966)
  Pallas kernels: 55 us -> 53.1 us
    pallas_call x1, Pallas kernels: 53.2 us -> 51.1 us  [body(): pl.pallas_call(functools.partial(kernel, nc, nz, names), out_shape=outs +...]
where the time goes in v4:
time: 53.9 us; the launch traced here: 53.8 us
  Pallas kernels  53.1 us (99%)
  between operations  0.64 us (1%)
    pallas_call x1, Pallas kernels, body(): pl.pallas_call(functools.partial(kernel, nc, nz, names), out_shape=outs +...  51.1 us
    pallas_call x1, Pallas kernels, body(): pl.pallas_call(place, out_shape=outs, in_specs=[pl.BlockSpec(memory_space...  1.96 us

profile of v4, /device:TPU:1, one launch (start us, length us, event | category | flops | bytes accessed | tf_op | source)
XLA Modules:
  0.0 53.8 jit_solution(5324616748384660000)
XLA Ops:
  0.6 51.1 %shard_map.165 = (f32[4,8192]{1,0:T(4,128)}, f32[4,6400]{1,0:T(4,128)}, f32[4,8192]{1,0:T(4,128)}, f32[4,6400]{1,0:T(4,128)}, f32[4,8192]{1,0:T(4,128)}, /*index=5*/f32[4,6400]{1,0:T(4,128)}, f32[8,128]{1,0:T(8,128)}) custom-call(f32[4,8192]{1,0:T(4,128)} %refs_0_.1, f32[4,6400]{1,0:T(4,128)} %refs_1_.1, f32[1,8192]{1,0:T(1,128)} %bitcast.5, ...), custom_call_target="tpu_custom_call" | custom-call | flops 4000000000 | bytes 10000000 | tf_op jit(solution)/shard_map/pallas_call | solution.py:679
  51.8 2.0 %shard_map.166 = (f32[4,8192]{1,0:T(4,128)}, f32[4,6400]{1,0:T(4,128)}, f32[4,8192]{1,0:T(4,128)}, f32[4,6400]{1,0:T(4,128)}) custom-call(f32[4,8192]{1,0:T(4,128)} %get-tuple-element.11.sol_a, f32[4,6400]{1,0:T(4,128)} %get-tuple-element.12.sol_s, f32[4,8192]{1,0:T(4,128)} %get-tuple-element.13.left_a, f32[4,6400]{1,0:T(4,128)} %get-tuple-element.14.left_s, ...), custom_call_target="tpu_custom_call" | custom-call | tf_op jit(solution)/shard_map/pallas_call | solution.py:688

commit v5 on v4

--- a/solution.py
+++ b/solution.py
@@ -133,14 +133,18 @@
         ny = min(4, nc // 2)
         nx = nc // (2 * ny)
         x, y, core = c // (2 * ny), c // 2 % ny, c % 2
-        xs = [lax.rem(x + (i + nx // 2) % nx, nx) * (2 * ny) for i in range(nx)]
-        ys = [lax.rem(y + (i + ny // 2) % ny, ny) * 2 for i in range(ny)]
-        cores = [core, 1 - core]
-        for i in range(nx):
+        ys = [lax.rem(y + (j + ny // 2) % ny, ny) * 2 for j in range(ny)]
+
+        @pl.loop(0, nx)
+        def _(i):
+            to_x = lax.rem(x + i + nx // 2, nx) * (2 * ny)
             for j in range(ny):
-                for k in range(2):
-                    if (i + nx // 2) % nx or (j + ny // 2) % ny or k:
-                        act(xs[i] + ys[j] + cores[k])
+                for to_core in (core, 1 - core):
+                    other = to_x + ys[j] + to_core
+                    if to_core is core and (j + ny // 2) % ny == 0:
+                        pl.when(other != c)(functools.partial(act, other))
+                    else:
+                        act(other)
 
     def to_cohort(src, dst, send_sem, recv_sem):
         around(lambda other: send(src, dst, send_sem, recv_sem, (other, z)))
@@ -253,14 +257,14 @@
     def slots_of(block):
         return jnp.concatenate([block[i : i + TRAITS, :] for i in range(0, prow, TRAITS)], axis=1)
 
-    readers = (((-2, 4), (-1, 3)), ((1, 0), (-1, 5)), ((2, 2), (1, 1)))
+    readers = (((-2, 5), (-1, 3)), ((1, 0), (-1, 4)), ((2, 1), (1, 2)))
 
     def send_sums_up(step, l):
         def to(readers_l):
             for offset, place_there in readers_l:
                 send(
                     r.up_own.at[step, l], r.up_recv.at[step, place_there],
-                    r.up_ssem.at[step], r.up_rsem.at[step], (cohort_at(offset), z),
+                    r.up_ssem.at[step], r.up_rsem.at[step, place_there // 2], (cohort_at(offset), z),
                 )
 
         if isinstance(l, int):
@@ -293,7 +297,9 @@
             marker_product(0)
             load_field(0, whole)
 
-            for l in reversed(range(SPAN)):
+            @pl.loop(0, SPAN)
+            def _(i):
+                l = SPAN - 1 - i
                 wait(r.idx_recv.at[l], r.idx_rsem.at[l])
                 for k in range(2):
                     hot, key = one_hot(r.idx_recv[l, k])
@@ -307,23 +313,25 @@
             r.hot_g[...] = hot
             r.key_g[...] = key
         else:
+            @pl.when(is_owner)
+            def _():
+                wait(r.z_s.at[1, :, pl.ds(0, (owners - 1) * OWN)], r.zs_rsem)
+
+            @pl.when(jnp.logical_not(is_owner))
+            def _():
+                wait(r.z_s.at[1], r.zs_rsem)
+
+            marker_product(1)
+
             wait(r.field.at[1, pl.ds(0, rows - prow), :], r.fl_rsem)
             load_field(1, whole)
 
-            for l in reversed(range(SPAN)):
+            @pl.loop(0, SPAN)
+            def _(i):
+                l = SPAN - 1 - i
                 total = gather_all(whole, l)
                 r.up_own[1, l] = halves(total)
                 send_sums_up(1, l)
-
-            @pl.when(is_owner)
-            def _():
-                wait(r.z_s.at[1, :, pl.ds(0, (owners - 1) * OWN)], r.zs_rsem)
-
-            @pl.when(jnp.logical_not(is_owner))
-            def _():
-                wait(r.z_s.at[1], r.zs_rsem)
-
-            marker_product(1)
 
             to_snp(
                 lambda k: r.image_a, lambda k: r.q_a.at[:, my_slots], r.qa_ssem, lambda k: r.qa_rsem, order
@@ -363,26 +371,28 @@
                         r.sum_s.at[step, c], r.ss_ssem.at[step], r.ss_rsem.at[step], (other, z),
                     )
 
+            if step == 0:
+                around(send_sums)
             return mismatch, tied, send_sums
 
         if step == 0:
             mismatch, tied, send_sums = tie_up()
 
         wait(r.own_recv.at[step], r.own_rsem.at[step])
-        wait(r.up_recv.at[step], r.up_rsem.at[step])
-        others = ((0, 2), (1, 3), (5, 4))
-        for l in range(SPAN):
-            parents = r.up_own[step, l] + r.up_recv[step, others[l][0]] + r.up_recv[step, others[l][1]]
+        def form(l):
+            wait(r.up_recv.at[step, pl.ds(0, 2)], r.up_rsem.at[step, l])
+            parents = r.up_own[step, l] + r.up_recv[step, 2 * l] + r.up_recv[step, 2 * l + 1]
             apart_l = r.own_recv[step, l] - 0.5 * parents
             mixed_l = mix(gen_inv, r.factor[l] * apart_l)
             r.terms[l] = -0.5 * mixed_l
-            if l == 0:
-                deviation, mixed = apart_l, mixed_l
-                r.mixed[step] = mixed
-                send(
-                    r.mixed.at[step], r.down_recv.at[step],
-                    r.down_ssem.at[step], r.down_rsem.at[step], (cohort_at(1), z),
-                )
+            return apart_l, mixed_l
+
+        deviation, mixed = form(0)
+        r.mixed[step] = mixed
+        send(
+            r.mixed.at[step], r.down_recv.at[step],
+            r.down_ssem.at[step], r.down_rsem.at[step], (cohort_at(1), z),
+        )
 
         own = r.z_a0[:, my_slots] if step == 0 else r.y_own[...]
         local_a = r.weight[...] * mix(res_inv, own)
@@ -421,6 +431,10 @@
 
         @pl.loop(0, SPAN)
         def _(l):
+            @pl.when(l > 0)
+            def _():
+                form(l)
+
             r.acc_b[...] += scatter(whole, r.terms[l], r.hot[2 * l], r.key[2 * l]) + scatter(
                 whole, r.terms[l], r.hot[2 * l + 1], r.key[2 * l + 1]
             )
@@ -434,7 +448,7 @@
 
         if step == 1:
             mismatch, tied, send_sums = tie_up()
-        around(send_sums)
+            around(send_sums)
         def send_dots():
             if step == 0:
                 r.mismatch[...] = mismatch
@@ -449,6 +463,33 @@
 
         if step == 1:
             send_dots()
+
+        def markers():
+            @pl.when(is_owner)
+            def _():
+                wait(r.sum_s.at[step, pl.ds(0, nc - 1)], r.ss_rsem.at[step])
+
+            image_s = local_s - jnp.sum(jnp.where(is_owner, r.sum_s[step], 0.0), axis=0)
+            if step == 0:
+                r.image_s[...] = image_s
+                y_s = precond_s(image_s, own_at)
+
+                @pl.when(is_owner)
+                def _():
+                    r.z_s[1, :, own_at] = y_s
+                    mine = r.z_s.at[1, :, own_at]
+                    to_cohort(mine, mine, r.zs_ssem, r.zs_rsem)
+            else:
+
+                @pl.when(is_owner)
+                def _():
+                    r.ws_own[...] = image_s
+                    landing = r.out_w_s.at[:, own_at]
+                    to_cohort(r.ws_own, landing, r.rs_ssem, r.rs_rsem)
+                    pltpu.make_async_copy(r.ws_own, landing, r.out_sem.at[6]).start()
+
+        if step == 0:
+            markers()
 
         tie = scatter((reach * prow, prow), tied, r.hot_g[...], r.key_g[...])
         local_a = local_a + slots_of(tie[0:prow, :] + tie[prow : 2 * prow, :])
@@ -479,28 +520,8 @@
             to_snp(lambda k: r.w_own, lambda k: landing, r.ra_ssem, lambda k: r.ra_rsem, order)
             pltpu.make_async_copy(r.w_own, landing, r.out_sem.at[5]).start()
 
-        @pl.when(is_owner)
-        def _():
-            wait(r.sum_s.at[step, pl.ds(0, nc - 1)], r.ss_rsem.at[step])
-
-        image_s = local_s - jnp.sum(jnp.where(is_owner, r.sum_s[step], 0.0), axis=0)
-        if step == 0:
-            r.image_s[...] = image_s
-            y_s = precond_s(image_s, own_at)
-
-            @pl.when(is_owner)
-            def _():
-                r.z_s[1, :, own_at] = y_s
-                mine = r.z_s.at[1, :, own_at]
-                to_cohort(mine, mine, r.zs_ssem, r.zs_rsem)
-        else:
-
-            @pl.when(is_owner)
-            def _():
-                r.ws_own[...] = image_s
-                landing = r.out_w_s.at[:, own_at]
-                to_cohort(r.ws_own, landing, r.rs_ssem, r.rs_rsem)
-                pltpu.make_async_copy(r.ws_own, landing, r.out_sem.at[6]).start()
+        if step == 1:
+            markers()
 
     wait(r.dot_c.at[1, pl.ds(0, nc - 1)], r.dc_rsem.at[1])
     dots = jnp.sum(r.dot_c[1], axis=0)
@@ -668,10 +689,11 @@
         load_sem=dma((11 + chunks,)),
     )
     for name, shape in dict(
-        idx=(SPAN,), up=(2,), own=(2,), down=(2,), mk=(2,), ss=(2,), dz=(2,), dc=(2,), bk=(2,), zs=(), rs=(), qs=(), qa=(), fl=(), ra=(),
+        idx=(SPAN,), own=(2,), down=(2,), mk=(2,), ss=(2,), dz=(2,), dc=(2,), bk=(2,), zs=(), rs=(), qs=(), qa=(), fl=(), ra=(),
     ).items():
         scratch[name + "_ssem"] = dma(shape)
         scratch[name + "_rsem"] = dma(shape)
+    scratch |= dict(up_ssem=dma((2,)), up_rsem=dma((2, SPAN)))
     names = ["in_" + name for name in inputs]
     names += ["out_sol_a", "out_sol_s", "out_left_a", "out_left_s", "out_w_a", "out_w_s", "out_scale"] + list(scratch)
     outs = [jax.ShapeDtypeStruct(x.shape, F32) for x in (rhs_a, rhs_s, rhs_a, rhs_s)]

time: 53.9 us -> 52.2 us (0.968)
  Pallas kernels: 53.1 us -> 51.4 us
    pallas_call x1, Pallas kernels: 51.1 us -> 49.5 us  [body(): pl.pallas_call(functools.partial(kernel, nc, nz, names), out_shape=outs +...]
where the time goes in v5:
time: 52.2 us; the launch traced here: 52.1 us
  Pallas kernels  51.4 us (98%)
  between operations  0.64 us (1%)
    pallas_call x1, Pallas kernels, body(): pl.pallas_call(functools.partial(kernel, nc, nz, names), out_shape=outs +...  49.5 us
    pallas_call x1, Pallas kernels, body(): pl.pallas_call(place, out_shape=outs, in_specs=[pl.BlockSpec(memory_space...  1.96 us

profile of v5, /device:TPU:1, one launch (start us, length us, event | category | flops | bytes accessed | tf_op | source)
XLA Modules:
  0.0 52.1 jit_solution(16246442091685077192)
XLA Ops:
  0.6 49.5 %shard_map.165 = (f32[4,8192]{1,0:T(4,128)}, f32[4,6400]{1,0:T(4,128)}, f32[4,8192]{1,0:T(4,128)}, f32[4,6400]{1,0:T(4,128)}, f32[4,8192]{1,0:T(4,128)}, /*index=5*/f32[4,6400]{1,0:T(4,128)}, f32[8,128]{1,0:T(8,128)}) custom-call(f32[4,8192]{1,0:T(4,128)} %refs_0_.1, f32[4,6400]{1,0:T(4,128)} %refs_1_.1, f32[1,8192]{1,0:T(1,128)} %bitcast.5, ...), custom_call_target="tpu_custom_call" | custom-call | flops 4000000000 | bytes 10000000 | tf_op jit(solution)/shard_map/pallas_call | solution.py:701
  50.1 2.0 %shard_map.166 = (f32[4,8192]{1,0:T(4,128)}, f32[4,6400]{1,0:T(4,128)}, f32[4,8192]{1,0:T(4,128)}, f32[4,6400]{1,0:T(4,128)}) custom-call(f32[4,8192]{1,0:T(4,128)} %get-tuple-element.11.sol_a, f32[4,6400]{1,0:T(4,128)} %get-tuple-element.12.sol_s, f32[4,8192]{1,0:T(4,128)} %get-tuple-element.13.left_a, f32[4,6400]{1,0:T(4,128)} %get-tuple-element.14.left_s, ...), custom_call_target="tpu_custom_call" | custom-call | tf_op jit(solution)/shard_map/pallas_call | solution.py:710

commit v6 on v5

--- a/solution.py
+++ b/solution.py
@@ -326,9 +326,7 @@
             wait(r.field.at[1, pl.ds(0, rows - prow), :], r.fl_rsem)
             load_field(1, whole)
 
-            @pl.loop(0, SPAN)
-            def _(i):
-                l = SPAN - 1 - i
+            for l in reversed(range(SPAN)):
                 total = gather_all(whole, l)
                 r.up_own[1, l] = halves(total)
                 send_sums_up(1, l)

time: 52.2 us -> 52.1 us (level)
  no operation moved by 1% of the time
where the time goes in v6:
time: 52.1 us; the launch traced here: 52 us
  Pallas kernels  51.3 us (98%)
  between operations  0.64 us (1%)
    pallas_call x1, Pallas kernels, body(): pl.pallas_call(functools.partial(kernel, nc, nz, names), out_shape=outs +...  49.3 us
    pallas_call x1, Pallas kernels, body(): pl.pallas_call(place, out_shape=outs, in_specs=[pl.BlockSpec(memory_space...  1.96 us

profile of v6, /device:TPU:1, one launch (start us, length us, event | category | flops | bytes accessed | tf_op | source)
XLA Modules:
  0.0 52.0 jit_solution(6239624249662398193)
XLA Ops:
  0.6 49.3 %shard_map.165 = (f32[4,8192]{1,0:T(4,128)}, f32[4,6400]{1,0:T(4,128)}, f32[4,8192]{1,0:T(4,128)}, f32[4,6400]{1,0:T(4,128)}, f32[4,8192]{1,0:T(4,128)}, /*index=5*/f32[4,6400]{1,0:T(4,128)}, f32[8,128]{1,0:T(8,128)}) custom-call(f32[4,8192]{1,0:T(4,128)} %refs_0_.1, f32[4,6400]{1,0:T(4,128)} %refs_1_.1, f32[1,8192]{1,0:T(1,128)} %bitcast.5, ...), custom_call_target="tpu_custom_call" | custom-call | flops 4000000000 | bytes 10000000 | tf_op jit(solution)/shard_map/pallas_call | solution.py:699
  50.0 2.0 %shard_map.166 = (f32[4,8192]{1,0:T(4,128)}, f32[4,6400]{1,0:T(4,128)}, f32[4,8192]{1,0:T(4,128)}, f32[4,6400]{1,0:T(4,128)}) custom-call(f32[4,8192]{1,0:T(4,128)} %get-tuple-element.11.sol_a, f32[4,6400]{1,0:T(4,128)} %get-tuple-element.12.sol_s, f32[4,8192]{1,0:T(4,128)} %get-tuple-element.13.left_a, f32[4,6400]{1,0:T(4,128)} %get-tuple-element.14.left_s, ...), custom_call_target="tpu_custom_call" | custom-call | tf_op jit(solution)/shard_map/pallas_call | solution.py:708
